TPU v7x, 256 devices: a whole 4x4x8 slice. The times are simulated.
256 devices in a mesh: half: 4 (over z_lo, core), gz: 64 (over x, y, z_hi).
Axes of the slice: x: 4, y: 4, z: 8 (z_hi: 4, z_lo: 2; z = z_hi * 2 + z_lo), core: 2. Of those that a mesh axis runs over, the one named last changes fastest.
Arguments:
- density: float32 [4, 256, 4, 2048], P('half', 'gz'), may hold values from -6 to 6
- lift_weight: float32 [16], replicated, may hold values from -3 to 3
- lift_bias: float32 [16], replicated, may hold values from -1 to 1
- conv_first: bfloat16 [16, 16, 3, 3, 3], replicated, may hold values from -0.3125 to 0.3125
- bias_first: float32 [16], replicated, may hold values from -1 to 1
- conv_second: bfloat16 [16, 16, 3, 3, 3], replicated, may hold values from -0.3125 to 0.3125
- bias_second: float32 [16], replicated, may hold values from -1 to 1
- projection: float32 [16], replicated, may hold values from -1.5 to 1.5
- wedge: float32 [256, 2048], replicated, may hold values from 0.1 to 1
Outputs:
- residual: float32 [4, 256, 4, 2048], P('half', 'gz')
All inputs are finite; a program needn't handle non-finite values.
Results may differ from a plain program's by a relative error of at most 0.04.
Values may be sent and summed in bfloat16 or wider, within the bound.
No kernel may reach another device: no remote copies, remote signals or barrier semaphores. Data moves between devices by JAX's collectives and lax.ppermute only.
A program may use at most 128 MiB of HBM per device.

v0:
```python
import math

import jax
import jax.numpy as jnp
from jax import lax
from jax.sharding import PartitionSpec as P


def extended(cells, sides, width):
    for axis, dim in sides:
        count = lax.axis_size(axis)
        ends = count - 1
        head = lax.slice_in_dim(cells, 0, width, axis=dim)
        tail = lax.slice_in_dim(cells, cells.shape[dim] - width, cells.shape[dim], axis=dim)
        cells = jnp.concatenate(
            [
                lax.ppermute(tail, axis, [(i, (i + 1) % count) for i in range(ends)]),
                cells,
                lax.ppermute(head, axis, [((i + 1) % count, i) for i in range(ends)]),
            ],
            axis=dim,
        )
    return cells


def from_partner(shard, axis, apart):
    return lax.ppermute(shard, axis, [(i, i ^ 1 << apart) for i in range(lax.axis_size(axis))])


def tables(count, first, size):
    rows_idx = jnp.arange(size, dtype=jnp.int32)[:, None]
    cols_idx = first + jnp.arange(count, dtype=jnp.int32)[None, :]
    product = rows_idx * cols_idx % size
    angle = product.astype(jnp.float32) * (2.0 * math.pi / size)
    return (jnp.cos(angle).astype(jnp.bfloat16), jnp.sin(angle).astype(jnp.bfloat16))


def convolve(feat, kernel):
    out = lax.conv_general_dilated(
        feat[None],
        kernel,
        (1, 1, 1),
        ((0, 0), (1, 1), (1, 1)),
        dimension_numbers=("NCDHW", "OIDHW", "NCDHW"),
        preferred_element_type=jnp.float32,
    )
    return out[0]


def lift_cells(values, lift_weight, lift_bias):
    return jax.nn.silu(
        lift_weight[:, None, None, None] * values[None] + lift_bias[:, None, None, None]
    ).astype(jnp.bfloat16)


def add_margin(feat):
    return extended(feat, (("gz", 1),), 1)


def inverse_rows(slab_re, slab_im, cols_x, block, blocks):

    def inverse_block(index, buffer):
        cos_b, sin_b = tables(block, index * block, cols_x)
        part = jnp.dot(slab_re, cos_b, preferred_element_type=jnp.float32) - jnp.dot(
            slab_im, sin_b, preferred_element_type=jnp.float32
        )
        return lax.dynamic_update_slice(buffer, part, (0, index * block))

    return lax.fori_loop(
        0, blocks, inverse_block, jnp.zeros((slab_re.shape[0], cols_x), jnp.float32)
    )


def body(
    density,
    lift_weight,
    lift_bias,
    conv_first,
    bias_first,
    conv_second,
    bias_second,
    projection,
    wedge,
):
    slab = density[0]
    depth, rows_y, cols_x = slab.shape
    devices_z = lax.axis_size("gz")
    total_z = depth * devices_z
    lifted = lift_cells(slab, lift_weight, lift_bias)
    hidden = jax.nn.silu(
        convolve(add_margin(lifted), conv_first) + bias_first[:, None, None, None]
    ).astype(jnp.bfloat16)
    second = convolve(add_margin(hidden), conv_second)
    activated = jax.nn.silu(second + bias_second[:, None, None, None])
    mixed = (slab + jnp.einsum("c,czyx->zyx", projection, activated)).astype(jnp.bfloat16)
    rows_all = depth * rows_y
    flat = mixed.reshape(rows_all, cols_x)
    block = min(cols_x, 512)
    blocks = cols_x // block

    def forward_block(index, buffer):
        cos_b, sin_b = tables(block, index * block, cols_x)
        part_re = jnp.dot(flat, cos_b, preferred_element_type=jnp.float32)
        part_im = -jnp.dot(flat, sin_b, preferred_element_type=jnp.float32)
        stacked = jnp.stack([part_re, part_im]).astype(jnp.bfloat16)
        return lax.dynamic_update_slice(buffer, stacked, (0, 0, index * block))

    spectrum = lax.fori_loop(
        0, blocks, forward_block, jnp.zeros((2, rows_all, cols_x), jnp.bfloat16)
    )
    spectrum = spectrum.reshape(2, depth, rows_y * cols_x)
    pencils = lax.all_to_all(spectrum, "gz", split_axis=2, concat_axis=1, tiled=True)
    columns = pencils.shape[2]
    start = lax.axis_index("gz") * columns
    weights = lax.dynamic_slice_in_dim(wedge, start % cols_x, columns, 1)
    cos_z, sin_z = tables(total_z, 0, total_z)
    spec_re = pencils[0]
    spec_im = pencils[1]
    freq_re = jnp.dot(cos_z, spec_re, preferred_element_type=jnp.float32) + jnp.dot(
        sin_z, spec_im, preferred_element_type=jnp.float32
    )
    freq_im = jnp.dot(cos_z, spec_im, preferred_element_type=jnp.float32) - jnp.dot(
        sin_z, spec_re, preferred_element_type=jnp.float32
    )
    weighted = jnp.stack([freq_re * weights, freq_im * weights]).astype(jnp.bfloat16)
    other = from_partner(weighted, "half", 0)
    diff = (weighted.astype(jnp.float32) - other.astype(jnp.float32)).astype(jnp.bfloat16)
    diff_re = diff[0]
    diff_im = diff[1]
    back_re = jnp.dot(cos_z, diff_re, preferred_element_type=jnp.float32) - jnp.dot(
        sin_z, diff_im, preferred_element_type=jnp.float32
    )
    back_im = jnp.dot(cos_z, diff_im, preferred_element_type=jnp.float32) + jnp.dot(
        sin_z, diff_re, preferred_element_type=jnp.float32
    )
    returned = jnp.stack([back_re, back_im]).astype(jnp.bfloat16)
    slabs = lax.all_to_all(returned, "gz", split_axis=1, concat_axis=2, tiled=True)
    slabs = slabs.reshape(2, rows_all, cols_x)
    scale = 1.0 / (cols_x * total_z)
    result = inverse_rows(slabs[0], slabs[1], cols_x, block, blocks) * scale
    return result.reshape(depth, rows_y, cols_x)[None]


def solution(mesh):
    placed = (P("half", "gz", None, None), P(), P(), P(), P(), P(), P(), P(), P())
    return jax.shard_map(
        body, mesh=mesh, in_specs=placed, out_specs=P("half", "gz", None, None), check_vma=False
    )
```

profile of v0, /device:TPU:1, one launch (start us, length us, event | category | flops | bytes accessed | tf_op | source)
XLA Modules:
  0.0 519.8 jit_solution(12459362671669330344)
XLA Ops:
  0.0 1.6 multiply_convert_fusion.1
  1.7 5.7 %collective-permute-start = (bf16[16,1,4,2048]{3,0,2,1:T(8,128)(2,1)S(1)}, bf16[16,1,4,2048]{3,0,2,1:T(8,128)(2,1)S(1)}, u32[]{:S(2)}, u32[]{:S(2)}) collective-permute-start(bf16[16,1,4,2048]{3,0,2,1:T(8,128)(2,1)S(1)} %get-tuple-element.223), channel_id=1, source_target_pairs={{0,1},{1,2},{2,3},{3,4},{4,5},{5,6},{6,7},{7,8},{8,9},{9,10},{10,1... | collective-permute-start | bytes 786440 | tf_op jit(solution)/shard_map/ppermute | solution.py:17
  7.5 1.3 collective-permute-start.1
  8.8 4.6 collective-permute-done
  13.4 12.1 %collective-permute-done.1 = bf16[16,1,4,2048]{3,0,2,1:T(8,128)(2,1)S(1)} collective-permute-done((bf16[16,1,4,2048]{3,0,2,1:T(8,128)(2,1)S(1)}, bf16[16,1,4,2048]{3,0,2,1:T(8,128)(2,1)S(1)}, u32[]{:S(2)}, u32[]{:S(2)}) %collective-permute-start.1) | collective-permute-done | bytes 262176 | tf_op jit(solution)/shard_map/ppermute | solution.py:19
  25.5 0.2 maximum_bitcast_fusion
  25.6 1.9 pad
  27.5 4.2 reshape.34
  31.8 10.9 %copy.46 = bf16[16,6,4,1,8,257]{0,4,5,2,1,3:T(8,128)(2,1)} copy(bf16[16,6,4,1,8,257]{5,4,0,2,1,3:T(8,128)(2,1)S(1)} %reshape.34) | data formatting | bytes 3158016 | tf_op jit(solution)/shard_map/conv_general_dilated | solution.py:39
  42.7 0.9 slice.50
  43.6 29.8 %fusion.63 = f32[4,4,8,257,16]{4,2,3,1,0:T(8,128)} fusion(bf16[16,16,3,3,3]{1,0,4,3,2:T(8,128)(2,1)S(1)} %copy-done, bf16[16,6,4,1,7,2]{0,4,5,2,1,3:T(8,128)(2,1)S(1)} %slice.50, bf16[16,6,4,1,8,257]{0,4,5,2,1,3:T(8,128)(2,1)} %copy.46, pred[8,257]{0,1:T(8,128)(4,1)S(1)} %copy-done.7), kind=kOutput, calls=%fused_computation.69 | convolution fusion | flops 384262144 | bytes 3710984 | tf_op jit(solution)/shard_map/conv_general_dilated | solution.py:39
  73.4 11.2 %copy.47 = f32[4,4,8,257,16]{3,2,4,1,0:T(8,128)S(1)} copy(f32[4,4,8,257,16]{4,2,3,1,0:T(8,128)} %fusion.63) | data formatting | bytes 4210688 | tf_op jit(solution)/shard_map/conv_general_dilated | solution.py:39
  84.7 1.9 reshape.38
  86.6 2.2 multiply_convert_fusion
  88.9 5.3 %collective-permute-start.2 = (bf16[16,1,4,2048]{3,0,2,1:T(8,128)(2,1)S(1)}, bf16[16,1,4,2048]{3,0,2,1:T(8,128)(2,1)S(1)}, u32[]{:S(2)}, u32[]{:S(2)}) collective-permute-start(bf16[16,1,4,2048]{3,0,2,1:T(8,128)(2,1)S(1)} %get-tuple-element.221), channel_id=1, source_target_pairs={{0,1},{1,2},{2,3},{3,4},{4,5},{5,6},{6,7},{7,8},{8,9},{9,10},{10,1... | collective-permute-start | bytes 786440 | tf_op jit(solution)/shard_map/ppermute | solution.py:17
  94.2 1.5 collective-permute-start.3
  95.7 7.5 %collective-permute-done.2 = bf16[16,1,4,2048]{3,0,2,1:T(8,128)(2,1)S(1)} collective-permute-done((bf16[16,1,4,2048]{3,0,2,1:T(8,128)(2,1)S(1)}, bf16[16,1,4,2048]{3,0,2,1:T(8,128)(2,1)S(1)}, u32[]{:S(2)}, u32[]{:S(2)}) %collective-permute-start.2) | collective-permute-done | bytes 262176 | tf_op jit(solution)/shard_map/ppermute | solution.py:17
  103.2 1.9 collective-permute-done.3
  105.3 1.9 pad.2
  107.2 4.2 reshape.41
  111.4 10.9 %copy.49 = bf16[16,6,4,1,8,257]{0,4,5,2,1,3:T(8,128)(2,1)} copy(bf16[16,6,4,1,8,257]{5,4,0,2,1,3:T(8,128)(2,1)S(1)} %reshape.41) | data formatting | bytes 3158016 | tf_op jit(solution)/shard_map/conv_general_dilated | solution.py:39
  122.3 0.9 slice.54
  123.3 29.8 %fusion.60 = f32[4,4,8,257,16]{4,2,3,1,0:T(8,128)} fusion(bf16[16,16,3,3,3]{1,0,4,3,2:T(8,128)(2,1)S(1)} %copy-done.4, bf16[16,6,4,1,7,2]{0,4,5,2,1,3:T(8,128)(2,1)S(1)} %slice.54, bf16[16,6,4,1,8,257]{0,4,5,2,1,3:T(8,128)(2,1)} %copy.49, pred[8,257]{0,1:T(8,128)(4,1)S(1)} %copy-done.7), kind=kOutput, calls=%fused_computation.68 | convolution fusion | flops 384262144 | bytes 3710984 | tf_op jit(solution)/shard_map/conv_general_dilated | solution.py:39
  153.1 11.2 %copy.50 = f32[4,4,8,257,16]{3,2,4,1,0:T(8,128)S(1)} copy(f32[4,4,8,257,16]{4,2,3,1,0:T(8,128)} %fusion.60) | data formatting | bytes 4210688 | tf_op jit(solution)/shard_map/conv_general_dilated | solution.py:39
  164.3 1.9 reshape.45
  166.2 2.4 fusion.70
  168.7 127.8 %while.30 = (s32[]{:T(128)}, bf16[2,16,2048]{2,1,0:T(8,128)(2,1)S(1)}, bf16[16,2048]{1,0:T(8,128)(2,1)S(1)}, s32[]{:T(128)}, s32[]{:T(128)}, /*index=5*/s32[]{:T(128)}, s32[]{:T(128)}) while((s32[]{:T(128)}, bf16[2,16,2048]{2,1,0:T(8,128)(2,1)S(1)}, bf16[16,2048]{1,0:T(8,128)(2,1)S(1)}, s32[]{:T(128)}, s32[]{:T(128)}, /*index=5*/s32[]{:T(128)}, ...), condition=%wide.region_1.2_spmd, body=%wide.region_0.1_spmd.sunk | while | flops 98656768 | bytes 235651 | solution.py:108
  169.0 16.0 %fusion.172 = bf16[1,16,512]{2,1,0:T(8,128)(2,1)S(1)} fusion(bf16[16,2048]{1,0:T(8,128)(2,1)S(1)} %get-tuple-element.289, s32[512]{0:T(512)S(1)} %iota_add_fusion.4), kind=kOutput, calls=%fused_computation.17.clone.1 | convolution fusion | flops 49299456 | bytes 83968 | tf_op jit(solution)/shard_map/while/body/eval_jaxpr/dot_general | solution.py:104
  185.0 15.9 %fusion.173 = bf16[1,16,512]{2,1,0:T(8,128)(2,1)S(1)} fusion(bf16[16,2048]{1,0:T(8,128)(2,1)S(1)} %get-tuple-element.289, s32[512]{0:T(512)S(1)} %iota_add_fusion.4), kind=kOutput, calls=%fused_computation.16.clone.1 | convolution fusion | flops 49291264 | bytes 83968 | tf_op jit(solution)/shard_map/while/body/eval_jaxpr/dot_general | solution.py:103
  200.9 16.0 %fusion.172 = bf16[1,16,512]{2,1,0:T(8,128)(2,1)S(1)} fusion(bf16[16,2048]{1,0:T(8,128)(2,1)S(1)} %get-tuple-element.289, s32[512]{0:T(512)S(1)} %iota_add_fusion.4), kind=kOutput, calls=%fused_computation.17.clone.1 | convolution fusion | flops 49299456 | bytes 83968 | tf_op jit(solution)/shard_map/while/body/eval_jaxpr/dot_general | solution.py:104
  216.9 15.9 %fusion.173 = bf16[1,16,512]{2,1,0:T(8,128)(2,1)S(1)} fusion(bf16[16,2048]{1,0:T(8,128)(2,1)S(1)} %get-tuple-element.289, s32[512]{0:T(512)S(1)} %iota_add_fusion.4), kind=kOutput, calls=%fused_computation.16.clone.1 | convolution fusion | flops 49291264 | bytes 83968 | tf_op jit(solution)/shard_map/while/body/eval_jaxpr/dot_general | solution.py:103
  232.8 16.0 %fusion.172 = bf16[1,16,512]{2,1,0:T(8,128)(2,1)S(1)} fusion(bf16[16,2048]{1,0:T(8,128)(2,1)S(1)} %get-tuple-element.289, s32[512]{0:T(512)S(1)} %iota_add_fusion.4), kind=kOutput, calls=%fused_computation.17.clone.1 | convolution fusion | flops 49299456 | bytes 83968 | tf_op jit(solution)/shard_map/while/body/eval_jaxpr/dot_general | solution.py:104
  248.8 15.9 %fusion.173 = bf16[1,16,512]{2,1,0:T(8,128)(2,1)S(1)} fusion(bf16[16,2048]{1,0:T(8,128)(2,1)S(1)} %get-tuple-element.289, s32[512]{0:T(512)S(1)} %iota_add_fusion.4), kind=kOutput, calls=%fused_computation.16.clone.1 | convolution fusion | flops 49291264 | bytes 83968 | tf_op jit(solution)/shard_map/while/body/eval_jaxpr/dot_general | solution.py:103
  264.7 16.0 %fusion.172 = bf16[1,16,512]{2,1,0:T(8,128)(2,1)S(1)} fusion(bf16[16,2048]{1,0:T(8,128)(2,1)S(1)} %get-tuple-element.289, s32[512]{0:T(512)S(1)} %iota_add_fusion.4), kind=kOutput, calls=%fused_computation.17.clone.1 | convolution fusion | flops 49299456 | bytes 83968 | tf_op jit(solution)/shard_map/while/body/eval_jaxpr/dot_general | solution.py:104
  280.7 15.9 %fusion.173 = bf16[1,16,512]{2,1,0:T(8,128)(2,1)S(1)} fusion(bf16[16,2048]{1,0:T(8,128)(2,1)S(1)} %get-tuple-element.289, s32[512]{0:T(512)S(1)} %iota_add_fusion.4), kind=kOutput, calls=%fused_computation.16.clone.1 | convolution fusion | flops 49291264 | bytes 83968 | tf_op jit(solution)/shard_map/while/body/eval_jaxpr/dot_general | solution.py:103
  296.7 6.9 %copy.51 = bf16[2,4,8192]{1,0,2:T(2,128)(2,1)} copy(bf16[2,4,8192]{2,1,0:T(4,128)(2,1)S(1)} %reshape.31) | data formatting | bytes 262144 | tf_op jit(solution)/shard_map/reshape | solution.py:111
  303.7 9.3 %reshape.58 = bf16[64,2,512]{2,1,0:T(2,128)(2,1)} reshape(bf16[8192,2,4]{2,1,0:T(2,128)(2,1)} %bitcast.135) | data formatting | bytes 262144
  313.0 12.8 %all-to-all-start = ((bf16[64,2,512]{2,1,0:T(2,128)(2,1)}), bf16[64,2,512]{2,1,0:T(2,128)(2,1)S(1)}, u32[]{:S(2)}, u32[]{:S(2)}) async-start(bf16[64,2,512]{2,1,0:T(2,128)(2,1)} %reshape.58), calls=%async_computation | async-start | bytes 262144 | tf_op jit(solution)/shard_map/all_to_all | solution.py:112
  325.8 11.5 %all-to-all-done = bf16[64,2,512]{2,1,0:T(2,128)(2,1)S(1)} async-done(((bf16[64,2,512]{2,1,0:T(2,128)(2,1)}), bf16[64,2,512]{2,1,0:T(2,128)(2,1)S(1)}, u32[]{:S(2)}, u32[]{:S(2)}) %all-to-all-start) | async-done | bytes 131104 | tf_op jit(solution)/shard_map/all_to_all | solution.py:112
  337.3 10.0 %reshape.59 = bf16[8192,2,4]{2,1,0:T(2,128)(2,1)} reshape(bf16[64,2,512]{2,1,0:T(2,128)(2,1)S(1)} %all-to-all-done) | data formatting | bytes 262144
  347.3 8.7 %copy.52 = bf16[2,4,64,128]{3,1,2,0:T(4,128)(2,1)S(1)} copy(bf16[2,4,64,128]{1,0,3,2:T(2,128)(2,1)} %bitcast.136) | data formatting | bytes 262144 | tf_op jit(solution)/shard_map/all_to_all | solution.py:112
  356.0 1.2 fusion.99
  357.2 1.2 fusion.98
  358.5 2.0 fusion.85
  360.5 2.0 fusion.86
  362.5 7.3 %collective-permute-start.4 = (bf16[2,256,128]{2,1,0:T(8,128)(2,1)S(1)}, bf16[2,256,128]{2,1,0:T(8,128)(2,1)S(1)}, u32[]{:S(2)}, u32[]{:S(2)}) collective-permute-start(bf16[2,256,128]{2,1,0:T(8,128)(2,1)S(1)} %pad_maximum_fusion), channel_id=1, source_target_pairs={{0,64},{64,0},{128,192},{192,128},{1,65},{65,1},{129,193},{193,129... | collective-permute-start | bytes 393224 | tf_op jit(solution)/shard_map/ppermute | solution.py:27
  369.8 1.0 collective-permute-done.4
  370.8 1.1 fusion.97
  371.9 1.1 fusion.96
  373.0 1.1 fusion.84
  374.1 1.1 fusion.83
  375.3 0.8 copy.53
  376.0 4.6 all-to-all-start.1
  380.7 11.9 %all-to-all-done.1 = bf16[2,256,128]{2,0,1:T(2,128)(2,1)S(1)} async-done(((bf16[2,256,128]{2,0,1:T(2,128)(2,1)}), bf16[2,256,128]{2,0,1:T(2,128)(2,1)S(1)}, u32[]{:S(2)}, u32[]{:S(2)}) %all-to-all-start.1) | async-done | bytes 131104 | tf_op jit(solution)/shard_map/all_to_all | solution.py:137
  392.9 125.8 %while.31 = (s32[]{:T(128)}, f32[16,2048]{1,0:T(8,128)S(1)}, bf16[16,2048]{1,0:T(8,128)(2,1)S(1)}, bf16[16,2048]{1,0:T(8,128)(2,1)S(1)}, s32[]{:T(128)}, /*index=5*/s32[]{:T(128)}, s32[]{:T(128)}, s32[]{:T(128)}) while((s32[]{:T(128)}, f32[16,2048]{1,0:T(8,128)S(1)}, bf16[16,2048]{1,0:T(8,128)(2,1)S(1)}, bf16[16,2048]{1,0:T(8,128)(2,1)S(1)}, ...), condition=%wide.region_3.4_spmd, body=%wide.region_2.3_spmd.sunk | while | flops 98574848 | bytes 235659 | solution.py:69
  393.1 15.4 %fusion.176 = f32[512,16]{0,1:T(8,128)S(1)} fusion(bf16[16,2048]{1,0:T(8,128)(2,1)S(1)} %get-tuple-element.312, s32[512]{0:T(512)S(1)} %iota_add_fusion.5), kind=kOutput, calls=%fused_computation.39.clone.1 | convolution fusion | flops 49283072 | bytes 100352 | tf_op jit(solution)/shard_map/while/body/eval_jaxpr/dot_general | solution.py:64
  408.5 16.0 %fusion.177 = f32[16,2048]{1,0:T(8,128)S(1)} fusion(f32[16,2048]{1,0:T(8,128)S(1)} %get-tuple-element.303, s32[]{:T(128)S(6)} %select_n.155, f32[512,16]{0,1:T(8,128)S(1)} %fusion.176, bf16[16,2048]{1,0:T(8,128)(2,1)S(1)} %get-tuple-element.313, s32[512]{0:T(512)S(1)} %iota_add_fusion.5), kind=kOutput, calls=%fused_computation.43.clone.1 | convolution fusion | flops 49291264 | bytes 133124 | tf_op jit(solution)/shard_map/while/body/eval_jaxpr/dot_general | solution.py:64
  424.5 15.4 %fusion.176 = f32[512,16]{0,1:T(8,128)S(1)} fusion(bf16[16,2048]{1,0:T(8,128)(2,1)S(1)} %get-tuple-element.312, s32[512]{0:T(512)S(1)} %iota_add_fusion.5), kind=kOutput, calls=%fused_computation.39.clone.1 | convolution fusion | flops 49283072 | bytes 100352 | tf_op jit(solution)/shard_map/while/body/eval_jaxpr/dot_general | solution.py:64
  439.9 16.0 %fusion.177 = f32[16,2048]{1,0:T(8,128)S(1)} fusion(f32[16,2048]{1,0:T(8,128)S(1)} %get-tuple-element.303, s32[]{:T(128)S(6)} %select_n.155, f32[512,16]{0,1:T(8,128)S(1)} %fusion.176, bf16[16,2048]{1,0:T(8,128)(2,1)S(1)} %get-tuple-element.313, s32[512]{0:T(512)S(1)} %iota_add_fusion.5), kind=kOutput, calls=%fused_computation.43.clone.1 | convolution fusion | flops 49291264 | bytes 133124 | tf_op jit(solution)/shard_map/while/body/eval_jaxpr/dot_general | solution.py:64
  455.9 15.4 %fusion.176 = f32[512,16]{0,1:T(8,128)S(1)} fusion(bf16[16,2048]{1,0:T(8,128)(2,1)S(1)} %get-tuple-element.312, s32[512]{0:T(512)S(1)} %iota_add_fusion.5), kind=kOutput, calls=%fused_computation.39.clone.1 | convolution fusion | flops 49283072 | bytes 100352 | tf_op jit(solution)/shard_map/while/body/eval_jaxpr/dot_general | solution.py:64
  471.3 16.0 %fusion.177 = f32[16,2048]{1,0:T(8,128)S(1)} fusion(f32[16,2048]{1,0:T(8,128)S(1)} %get-tuple-element.303, s32[]{:T(128)S(6)} %select_n.155, f32[512,16]{0,1:T(8,128)S(1)} %fusion.176, bf16[16,2048]{1,0:T(8,128)(2,1)S(1)} %get-tuple-element.313, s32[512]{0:T(512)S(1)} %iota_add_fusion.5), kind=kOutput, calls=%fused_computation.43.clone.1 | convolution fusion | flops 49291264 | bytes 133124 | tf_op jit(solution)/shard_map/while/body/eval_jaxpr/dot_general | solution.py:64
  487.3 15.4 %fusion.176 = f32[512,16]{0,1:T(8,128)S(1)} fusion(bf16[16,2048]{1,0:T(8,128)(2,1)S(1)} %get-tuple-element.312, s32[512]{0:T(512)S(1)} %iota_add_fusion.5), kind=kOutput, calls=%fused_computation.39.clone.1 | convolution fusion | flops 49283072 | bytes 100352 | tf_op jit(solution)/shard_map/while/body/eval_jaxpr/dot_general | solution.py:64
  502.7 16.0 %fusion.177 = f32[16,2048]{1,0:T(8,128)S(1)} fusion(f32[16,2048]{1,0:T(8,128)S(1)} %get-tuple-element.303, s32[]{:T(128)S(6)} %select_n.155, f32[512,16]{0,1:T(8,128)S(1)} %fusion.176, bf16[16,2048]{1,0:T(8,128)(2,1)S(1)} %get-tuple-element.313, s32[512]{0:T(512)S(1)} %iota_add_fusion.5), kind=kOutput, calls=%fused_computation.43.clone.1 | convolution fusion | flops 49291264 | bytes 133124 | tf_op jit(solution)/shard_map/while/body/eval_jaxpr/dot_general | solution.py:64
  518.7 0.7 broadcast_in_dim_reshape.3
  (46 shorter events, 1.2 us)
Async XLA Ops:
  0.0 43.6 %copy-start = (bf16[16,16,3,3,3]{1,0,4,3,2:T(8,128)(2,1)S(1)}, bf16[16,16,3,3,3]{1,0,4,3,2:T(8,128)(2,1)}, u32[]{:S(2)}) copy-start(bf16[16,16,3,3,3]{1,0,4,3,2:T(8,128)(2,1)} %param.16) | copy-start | bytes 41476
  1.7 11.7 %collective-permute-start = (bf16[16,1,4,2048]{3,0,2,1:T(8,128)(2,1)S(1)}, bf16[16,1,4,2048]{3,0,2,1:T(8,128)(2,1)S(1)}, u32[]{:S(2)}, u32[]{:S(2)}) collective-permute-start(bf16[16,1,4,2048]{3,0,2,1:T(8,128)(2,1)S(1)} %get-tuple-element.223), channel_id=1, source_target_pairs={{0,1},{1,2},{2,3},{3,4},{4,5},{5,6},{6,7},{7,8},{8,9},{9,10},{10,1... | collective-permute-start | bytes 786440 | tf_op jit(solution)/shard_map/ppermute | solution.py:17
  7.5 18.0 %collective-permute-start.1 = (bf16[16,1,4,2048]{3,0,2,1:T(8,128)(2,1)S(1)}, bf16[16,1,4,2048]{3,0,2,1:T(8,128)(2,1)S(1)}, u32[]{:S(2)}, u32[]{:S(2)}) collective-permute-start(bf16[16,1,4,2048]{3,0,2,1:T(8,128)(2,1)S(1)} %get-tuple-element.224), channel_id=1, source_target_pairs={{1,0},{2,1},{3,2},{4,3},{5,4},{6,5},{7,6},{8,7},{9,8},{10,9},{11,1... | collective-permute-start | bytes 786440 | tf_op jit(solution)/shard_map/ppermute | solution.py:19
  31.8 11.8 %copy-start.7 = (pred[8,257]{0,1:T(8,128)(4,1)S(1)}, pred[8,257]{0,1:T(8,128)(4,1)}, u32[]{:S(2)}) copy-start(pred[8,257]{0,1:T(8,128)(4,1)} %constant.183) | copy-start | bytes 6172
  84.7 1.9 copy-start.3
  88.9 14.3 %collective-permute-start.2 = (bf16[16,1,4,2048]{3,0,2,1:T(8,128)(2,1)S(1)}, bf16[16,1,4,2048]{3,0,2,1:T(8,128)(2,1)S(1)}, u32[]{:S(2)}, u32[]{:S(2)}) collective-permute-start(bf16[16,1,4,2048]{3,0,2,1:T(8,128)(2,1)S(1)} %get-tuple-element.221), channel_id=1, source_target_pairs={{0,1},{1,2},{2,3},{3,4},{4,5},{5,6},{6,7},{7,8},{8,9},{9,10},{10,1... | collective-permute-start | bytes 786440 | tf_op jit(solution)/shard_map/ppermute | solution.py:17
  94.2 10.9 %collective-permute-start.3 = (bf16[16,1,4,2048]{3,0,2,1:T(8,128)(2,1)S(1)}, bf16[16,1,4,2048]{3,0,2,1:T(8,128)(2,1)S(1)}, u32[]{:S(2)}, u32[]{:S(2)}) collective-permute-start(bf16[16,1,4,2048]{3,0,2,1:T(8,128)(2,1)S(1)} %get-tuple-element.222), channel_id=1, source_target_pairs={{1,0},{2,1},{3,2},{4,3},{5,4},{6,5},{7,6},{8,7},{9,8},{10,9},{11,1... | collective-permute-start | bytes 786440 | tf_op jit(solution)/shard_map/ppermute | solution.py:19
  111.4 11.8 %copy-start.4 = (bf16[16,16,3,3,3]{1,0,4,3,2:T(8,128)(2,1)S(1)}, bf16[16,16,3,3,3]{1,0,4,3,2:T(8,128)(2,1)}, u32[]{:S(2)}) copy-start(bf16[16,16,3,3,3]{1,0,4,3,2:T(8,128)(2,1)} %param.18) | copy-start | bytes 41476
  164.3 2.0 copy-start.5
  164.3 1.9 copy-start.6
  166.2 2.4 copy-start.2
  313.0 24.3 %all-to-all-start = ((bf16[64,2,512]{2,1,0:T(2,128)(2,1)}), bf16[64,2,512]{2,1,0:T(2,128)(2,1)S(1)}, u32[]{:S(2)}, u32[]{:S(2)}) async-start(bf16[64,2,512]{2,1,0:T(2,128)(2,1)} %reshape.58), calls=%async_computation | async-start | bytes 262144 | tf_op jit(solution)/shard_map/all_to_all | solution.py:112
  362.5 8.3 %collective-permute-start.4 = (bf16[2,256,128]{2,1,0:T(8,128)(2,1)S(1)}, bf16[2,256,128]{2,1,0:T(8,128)(2,1)S(1)}, u32[]{:S(2)}, u32[]{:S(2)}) collective-permute-start(bf16[2,256,128]{2,1,0:T(8,128)(2,1)S(1)} %pad_maximum_fusion), channel_id=1, source_target_pairs={{0,64},{64,0},{128,192},{192,128},{1,65},{65,1},{129,193},{193,129... | collective-permute-start | bytes 393224 | tf_op jit(solution)/shard_map/ppermute | solution.py:27
  376.0 16.5 %all-to-all-start.1 = ((bf16[2,256,128]{2,0,1:T(2,128)(2,1)}), bf16[2,256,128]{2,0,1:T(2,128)(2,1)S(1)}, u32[]{:S(2)}, u32[]{:S(2)}) async-start(bf16[2,256,128]{2,0,1:T(2,128)(2,1)} %copy.53), calls=%async_computation.1 | async-start | bytes 262144 | tf_op jit(solution)/shard_map/all_to_all | solution.py:137
  518.7 0.9 copy-start.1
where the time goes:
time: 528 us; the launch traced here: 520 us
  matrix products  326 us (62%)
  local copies, waits for them, and re-layouts  99.4 us (19%)
  waiting for transfers between devices  50.5 us (10%)
  starting transfers between devices  38.5 us (7%)
    dot_general x4, matrix products, forward_block(): part_im = -jnp.dot(flat, sin_b, preferred_element_type=jnp.float32)  64 us
    dot_general x4, matrix products, inverse_block(): jnp.dot(slab_im, sin_b, preferred_element_type=jnp.float32)  64 us
    dot_general x4, matrix products, forward_block(): part_re = jnp.dot(flat, cos_b, preferred_element_type=jnp.float32)  63.4 us
    dot_general x4, matrix products, inverse_block(): jnp.dot(slab_re, cos_b, preferred_element_type=jnp.float32)  61.6 us
    conv_general_dilated x2, matrix products, convolve(): lax.conv_general_dilated(feat[None], kernel, (1, 1, 1), ((0, 0), (1, 1),...  59.6 us
    conv_general_dilated x10, local copies, waits for them, and re-layouts, convolve(): lax.conv_general_dilated(feat[None], kernel, (1, 1, 1), ((0, 0), (1, 1),...  58.4 us
    unnamed x18, local copies, waits for them, and re-layouts  19.5 us
    ppermute x2, waiting for transfers between devices, extended(): lax.ppermute(head, axis, [((i + 1) % count, i) for i in range(ends)])  14 us
  transfers between devices with their start and end apart: 7, of which 7 were waited for; matrix products, arithmetic and copies ran while one was open for 0% of the time, Pallas kernels for 0%

commit v1 on v0

v1 whole, which is shorter than its diff:
```python
import math

import jax
import jax.numpy as jnp
import numpy as np
from jax import lax
from jax.experimental import pallas as pl
from jax.experimental.pallas import tpu as pltpu
from jax.sharding import PartitionSpec as P

NX, CH, NY, NZ = 2048, 16, 4, 256
GZ = 64
DEPTH = NZ // GZ
RADIX, INNER = 16, NX // 16
HALF = INNER // 2
BLOCKS = 16
LAG = 2
F32, BF16 = jnp.float32, jnp.bfloat16


def dot(a, b):
    return jnp.dot(a, b, preferred_element_type=F32)


def params(megabytes=8):
    return pltpu.CompilerParams(vmem_limit_bytes=megabytes << 20)


def turn(product, size):
    angle = 2.0 * math.pi * (product % size) / size
    return np.cos(angle), np.sin(angle)


def x_tables():
    x0 = np.arange(INNER)[:, None]
    k0 = np.arange(INNER)[None, :]
    c, s = turn(x0 * k0, INNER)
    pick = lambda t, h: t[:, h * HALF : (h + 1) * HALF]
    from_re = np.concatenate([pick(c, 0), pick(-s, 0), pick(c, 1), pick(-s, 1)], 1)
    from_im = np.concatenate([pick(s, 0), pick(c, 0), pick(s, 1), pick(c, 1)], 1)
    full = np.concatenate([from_re, from_im], 0)
    first = np.concatenate([pick(c, 0), pick(-s, 0)], 1)
    first[:, HALF] = c[:, HALF]
    c8, s8 = turn(x0 * (1 + 2 * np.arange(HALF)[None, :]), 2 * INNER)
    middle = np.concatenate([c8, -s8], 1)
    k1 = np.arange(1, 8)[:, None]
    ct, st = turn(k1 * np.arange(INNER)[None, :], NX)
    twiddle = np.concatenate([ct, np.zeros((1, INNER)), st, np.zeros((1, INNER))], 0)
    return (
        full.astype(jnp.bfloat16),
        np.concatenate([first, middle], 1).astype(jnp.bfloat16),
        full.T.astype(jnp.bfloat16),
        np.concatenate([first.T, middle.T], 1).astype(jnp.bfloat16),
        twiddle.astype(np.float32),
    )


def z_tables():
    kz = np.arange(NZ)[:, None]
    row = np.arange(NZ)[None, :]
    ahead = np.concatenate(turn(kz * (row - LAG), NZ), 0)
    back = np.concatenate(turn(kz * row, NZ), 0)
    return ahead.astype(jnp.bfloat16), back.astype(jnp.bfloat16)


def weights_kernel(edge_ref, first_ref, second_ref, w1_ref, w1m_ref, w2a_ref, w2b_ref):
    rows = lax.broadcasted_iota(jnp.int32, (128, 256), 0)
    cols = lax.broadcasted_iota(jnp.int32, (128, 256), 1)
    zo, yo = rows // 64, rows % 4
    zi, yi = cols // 64, cols % 4
    inner = edge_ref[0] == 0
    keep_mid = ((zi >= 2) == (zo == 1)) | inner
    keep_low = (zi <= 2) | inner
    keep_high = (zi >= 1) | inner
    spread_rows = (
        lax.broadcasted_iota(jnp.int32, (128, CH), 0) % 64 // 4
        == lax.broadcasted_iota(jnp.int32, (128, CH), 1)
    ).astype(F32).astype(BF16)
    spread_cols = (
        lax.broadcasted_iota(jnp.int32, (CH, 256), 1) % 64 // 4
        == lax.broadcasted_iota(jnp.int32, (CH, 256), 0)
    ).astype(F32).astype(BF16)
    place = (zi - zo) * 3 + (yi - yo + 1)
    valid = (yi - yo + 1 >= 0) & (yi - yo + 1 <= 2) & (zi - zo >= 0) & (zi - zo <= 2)
    place = jnp.where(valid, place, -1)
    for src, outs in (
        (first_ref, ((w1_ref, None), (w1m_ref, keep_mid))),
        (second_ref, ((w2a_ref, keep_low), (w2b_ref, keep_high))),
    ):
        wide = dot(src[...], spread_cols).astype(BF16)
        for e in range(3):
            total = jnp.zeros((128, 256), F32)
            for ab in range(9):
                at = (e * 9 + ab) * CH
                total = jnp.where(place == ab, dot(spread_rows, wide[at : at + CH]), total)
            total = total * 0.5
            for out, keep in outs:
                part = total if keep is None else jnp.where(keep, total, 0.0)
                out[:, e * 256 : (e + 1) * 256] = part.astype(BF16)


def silu_of_half(h):
    return h + h * jnp.tanh(h)


def filter_kernel(
    left_ref, own_ref, par_ref, w1_ref, w1m_ref, w2a_ref, w2b_ref, out_ref, x1, x2
):
    lane = lax.broadcasted_iota(jnp.int32, (16, NX), 1)
    at_start, at_end = lane == 0, lane == NX - 1

    def spread(ref, row, value):
        rows = pl.ds(row, 16)
        wide = value.astype(F32)
        ref[1, rows, :] = value
        ref[0, rows, :] = jnp.where(at_start, 0.0, pltpu.roll(wide, 1, 1)).astype(BF16)
        ref[2, rows, :] = jnp.where(at_end, 0.0, pltpu.roll(wide, NX - 1, 1)).astype(BF16)

    for z in range(2 * DEPTH):
        cells = left_ref[z] if z < DEPTH else own_ref[z - DEPTH]
        cells = jnp.concatenate([cells] * 4, axis=0)
        for block in range(4):
            gain = par_ref[block * 16 : block * 16 + 16, 0:1]
            shift = par_ref[block * 16 : block * 16 + 16, 1:2]
            lifted = silu_of_half(gain * cells + shift).astype(BF16)
            spread(x1, z * 64 + block * 16, lifted)

    chunk = 256

    def three(w_ref, x_ref, row, at):
        total = None
        for e in range(3):
            part = dot(w_ref[:, e * 256 : (e + 1) * 256], x_ref[e, row : row + 256, pl.ds(at, chunk)])
            total = part if total is None else total + part
        return total

    bias1 = par_ref[:, 2:3]
    bias1 = jnp.concatenate([bias1, bias1], 0)

    @pl.loop(0, NX // chunk)
    def _(index):
        at = pl.multiple_of(index * chunk, chunk)
        for g, w_ref in enumerate((w1_ref, w1m_ref, w1_ref)):
            pre = three(w_ref, x1, 128 * g, at) + bias1
            x2[1, 128 * g : 128 * g + 128, pl.ds(at, chunk)] = silu_of_half(pre).astype(BF16)

    @pl.loop(0, 24)
    def _(index):
        row = pl.multiple_of(index * 16, 16)
        spread(x2, row, x2[1, pl.ds(row, 16), :])

    bias2 = par_ref[:, 3:4]
    bias2 = jnp.concatenate([bias2, bias2], 0)
    mix = par_ref[:, 4:5]

    @pl.loop(0, NX // chunk)
    def _(index):
        at = pl.multiple_of(index * chunk, chunk)
        slices = []
        for g, w_ref in enumerate((w2a_ref, w2b_ref)):
            act = silu_of_half(three(w_ref, x2, 128 * g, at) + bias2)
            for zo in range(2):
                terms = act[zo * 64 : zo * 64 + 64] * mix
                total = terms[0:8]
                for pair in range(1, 8):
                    total = total + terms[pair * 8 : pair * 8 + 8]
                z = 2 + 2 * g + zo
                base = left_ref[z, :, pl.ds(at, chunk)] if z < DEPTH else own_ref[z - DEPTH, :, pl.ds(at, chunk)]
                slices.append(base + total[0:4] + total[4:8])
        mixed = jnp.concatenate([slices[z][y : y + 1] for y in range(NY) for z in range(DEPTH)], 0)
        out_ref[:, pl.ds(at, chunk)] = mixed.astype(BF16)


def cos16(n):
    return math.cos(2 * math.pi * (n % 16) / 16)


def sin16(n):
    return math.sin(2 * math.pi * (n % 16) / 16)


def weigh(terms):
    total = None
    for factor, value in terms:
        if abs(factor) < 1e-9:
            continue
        if abs(factor - 1) < 1e-9:
            term = value
        elif abs(factor + 1) < 1e-9:
            term = -value
        else:
            term = value * factor
        total = term if total is None else total + term
    return total


def forward_kernel(own_ref, other_ref, full_ref, ends_ref, twiddle_ref, out_ref):
    delta = own_ref[...].astype(F32) - other_ref[...].astype(F32)
    a = [delta[:, INNER * i : INNER * (i + 1)] for i in range(RADIX)]
    plus = [a[i] + a[16 - i] for i in range(1, 8)]
    minus = [a[i] - a[16 - i] for i in range(1, 8)]
    re, im = [], []
    for k1 in range(9):
        re.append(weigh([(1, a[0]), ((-1) ** k1, a[8])] + [(cos16(k1 * i), plus[i - 1]) for i in range(1, 8)]))
        im.append(weigh([(-sin16(k1 * i), minus[i - 1]) for i in range(1, 8)]))
    rows = []
    for k1 in range(1, 8):
        c, s = twiddle_ref[k1 - 1 : k1], twiddle_ref[k1 + 7 : k1 + 8]
        rows.append(jnp.concatenate([re[k1] * c + im[k1] * s, im[k1] * c - re[k1] * s], 1))
    whole = dot(jnp.concatenate(rows, 0).astype(BF16), full_ref[...])
    blocks = [
        dot(re[0].astype(BF16), ends_ref[:, :INNER]),
        dot(re[8].astype(BF16), ends_ref[:, INNER:]),
    ]
    for k1 in range(1, 8):
        for h in range(2):
            blocks.append(whole[(k1 - 1) * 16 : k1 * 16, h * INNER : (h + 1) * INNER])
    for y in range(NY):
        for b in range(BLOCKS):
            out_ref[y * BLOCKS + b] = blocks[b][y * DEPTH : (y + 1) * DEPTH].astype(BF16)


def inverse_kernel(in_ref, full_ref, ends_ref, twiddle_ref, out_ref):
    blocks = [
        jnp.concatenate([in_ref[y * BLOCKS + b].astype(F32) for y in range(NY)], 0).astype(BF16)
        for b in range(BLOCKS)
    ]
    even = dot(blocks[0], ends_ref[:, :INNER])
    mid = dot(blocks[1], ends_ref[:, INNER:])
    lows = jnp.concatenate([blocks[2 * k1] for k1 in range(1, 8)], 0)
    highs = jnp.concatenate([blocks[2 * k1 + 1] for k1 in range(1, 8)], 0)
    whole = dot(lows, full_ref[:INNER]) + dot(highs, full_ref[INNER:])
    re, im = [], []
    for k1 in range(1, 8):
        part = whole[(k1 - 1) * 16 : k1 * 16]
        b_re, b_im = part[:, :INNER], part[:, INNER:]
        c, s = twiddle_ref[k1 - 1 : k1], twiddle_ref[k1 + 7 : k1 + 8]
        re.append(b_re * c - b_im * s)
        im.append(b_re * s + b_im * c)
    scale = 1.0 / (NX * NZ)
    even, mid = even * scale, mid * scale
    re, im = [v * scale for v in re], [v * scale for v in im]
    out = [None] * RADIX
    for x1 in range(9):
        p = weigh([(1, even), ((-1) ** x1, mid)] + [(cos16(k1 * x1), re[k1 - 1]) for k1 in range(1, 8)])
        q = weigh([(sin16(k1 * x1), im[k1 - 1]) for k1 in range(1, 8)])
        if q is None:
            out[x1] = p
        else:
            out[x1], out[16 - x1] = p - q, p + q
    for x1 in range(RADIX):
        for z in range(DEPTH):
            rows = [out[x1][y * DEPTH + z : y * DEPTH + z + 1] for y in range(NY)]
            out_ref[z, :, x1 * INNER : (x1 + 1) * INNER] = jnp.concatenate(rows, 0)


def wedge_kernel(at_ref, wedge_ref, plus_ref, minus_ref):
    block = at_ref[0]
    k = lax.broadcasted_iota(jnp.int32, (NX, INNER), 0)
    j = lax.broadcasted_iota(jnp.int32, (NX, INNER), 1)
    col = j % HALF
    k1 = jnp.where(block == 0, 0, jnp.where(block == 1, 8, block // 2))
    high = jnp.where(block < 2, 0, block % 2)
    mine = k1 + RADIX * (HALF * high + col)
    target = jnp.where(j < HALF, mine, (NX - mine) % NX)
    special = (block == 0) & (col == 0)
    quarter = special & (k == NX // 2)
    hit = (k == target)
    plain = jnp.where(hit, jnp.where(special, 0.25, 1.0), 0.0) + jnp.where(quarter, 0.25, 0.0)
    cross = jnp.where(special, jnp.where(hit, 0.25, 0.0) - jnp.where(quarter, 0.25, 0.0), 0.0)
    select = jnp.concatenate([plain, cross], 1).astype(BF16)
    whole = wedge_ref[...]
    top = whole.astype(BF16)
    rest = (whole - top.astype(F32)).astype(BF16)
    picked = dot(top, select) + dot(rest, select)
    r = lax.broadcasted_iota(jnp.int32, (NZ, NZ), 0)
    c = lax.broadcasted_iota(jnp.int32, (NZ, NZ), 1)
    flip = ((r + c) % NZ == 0).astype(F32).astype(BF16)
    top = picked.astype(BF16)
    rest = (picked - top.astype(F32)).astype(BF16)
    turned = dot(flip, top) + dot(flip, rest)
    low = lax.broadcasted_iota(jnp.int32, (NZ, INNER), 1) < HALF
    for out, at in ((plus_ref, 0), (minus_ref, INNER)):
        here, there = picked[:, at : at + INNER], turned[:, at : at + INNER]
        both = jnp.where(low, here + pltpu.roll(there, HALF, 1), there + pltpu.roll(here, HALF, 1))
        out[...] = both


def middle_kernel(in_ref, plus_ref, minus_ref, ahead_ref, back_ref, out_ref):
    sign = jnp.where(lax.broadcasted_iota(jnp.int32, (NZ, INNER), 1) < HALF, 1.0, -1.0)
    both = dot(ahead_ref[...], in_ref[...])
    cos_part, sin_part = both[:NZ], pltpu.roll(both[NZ:], HALF, 1)
    freq = cos_part + sign * sin_part
    mirror = sign * cos_part - sin_part
    weighted = (plus_ref[...] * freq + minus_ref[...] * mirror).astype(BF16)
    both = dot(back_ref[...], weighted)
    out_ref[...] = (both[:NZ] - sign * pltpu.roll(both[NZ:], HALF, 1)).astype(BF16)


def call(kernel, outs, *args, scratch=(), megabytes=8, smem=0, flops=10**7):
    many = isinstance(outs, list)
    vmem = pl.BlockSpec(memory_space=pltpu.VMEM)
    scalar = pl.BlockSpec(memory_space=pltpu.SMEM)
    moved = sum(a.size * a.dtype.itemsize for a in args)
    return pl.pallas_call(
        kernel,
        out_shape=outs,
        in_specs=[scalar] * smem + [vmem] * (len(args) - smem),
        out_specs=[vmem] * len(outs) if many else vmem,
        scratch_shapes=scratch,
        compiler_params=params(megabytes),
        cost_estimate=pl.CostEstimate(flops=flops, bytes_accessed=moved, transcendentals=0),
    )(*args)


def shape(*dims, dtype=BF16):
    return jax.ShapeDtypeStruct(dims, dtype)


def body(
    density,
    lift_weight,
    lift_bias,
    conv_first,
    bias_first,
    conv_second,
    bias_second,
    projection,
    wedge,
):
    full_x, ends_x, full_i, ends_i, twiddle = x_tables()
    ahead, back = z_tables()
    place = lax.axis_index("gz")
    slab = density[0]
    left = lax.ppermute(slab, "gz", [(i, (i + 1) % GZ) for i in range(GZ)])

    edge = (place == 0).astype(jnp.int32).reshape(1)
    block = (place % BLOCKS).astype(jnp.int32).reshape(1)
    flat = lambda w: w.transpose(4, 2, 3, 0, 1).reshape(27 * CH, CH)
    weights = call(
        weights_kernel, [shape(128, 768)] * 4, edge, flat(conv_first), flat(conv_second),
        smem=1, megabytes=16, flops=10**9,
    )
    plus, minus = call(
        wedge_kernel, [shape(NZ, INNER, dtype=F32)] * 2, block, wedge,
        smem=1, megabytes=32, flops=10**9,
    )
    columns = jnp.stack(
        [0.5 * lift_weight, 0.5 * lift_bias, 0.5 * bias_first, 0.5 * bias_second, projection], 1
    )
    columns = jnp.repeat(columns, NY, axis=0)

    mixed = call(
        filter_kernel, shape(NY * DEPTH, NX), left, slab, columns, *weights,
        scratch=[pltpu.VMEM((3, 512, NX), BF16), pltpu.VMEM((3, 384, NX), BF16)],
        megabytes=40, flops=10**10,
    )
    other = lax.ppermute(mixed, "half", [(i, i ^ 1) for i in range(lax.axis_size("half"))])
    spectrum = call(
        forward_kernel, shape(GZ, DEPTH, INNER), mixed, other, full_x, ends_x, twiddle,
    )
    pencils = lax.all_to_all(spectrum, "gz", split_axis=0, concat_axis=0, tiled=True)
    returned = call(
        middle_kernel, shape(NZ, INNER), pencils.reshape(NZ, INNER), plus, minus, ahead, back,
    )
    slabs = lax.all_to_all(
        returned.reshape(GZ, DEPTH, INNER), "gz", split_axis=0, concat_axis=0, tiled=True
    )
    residual = call(
        inverse_kernel, shape(DEPTH, NY, NX, dtype=F32), slabs, full_i, ends_i, twiddle,
    )
    return residual[None]


def solution(mesh):
    placed = (P("half", "gz", None, None), P(), P(), P(), P(), P(), P(), P(), P())
    return jax.shard_map(
        body, mesh=mesh, in_specs=placed, out_specs=P("half", "gz", None, None), check_vma=False
    )
```

time: 528 us -> 68.1 us (0.13); the launches traced: 520 us -> 67.6 us
  matrix products: 326 us -> 0 us
  local copies, waits for them, and re-layouts: 99.4 us -> 2.67 us
  waiting for transfers between devices: 50.5 us -> 17 us
  starting transfers between devices: 38.5 us -> 14.4 us
  Pallas kernels: 0 us -> 16.7 us
  blocking collectives: 0 us -> 15.3 us
    dot_general x25 -> x0, matrix products: 266 us -> none  [the longest x4 64 us: forward_block(): part_im = -jnp.dot(flat, sin_b, preferred_element_type=jnp.float32)]
    conv_general_dilated x2 -> x0, matrix products: 59.6 us -> none  [convolve(): lax.conv_general_dilated(feat[None], kernel, (1, 1, 1), ((0, 0), (1, 1),...]
    conv_general_dilated x10 -> x0, local copies, waits for them, and re-layouts: 58.4 us -> none  [convolve(): lax.conv_general_dilated(feat[None], kernel, (1, 1, 1), ((0, 0), (1, 1),...]
    ppermute x5 -> x2, waiting for transfers between devices: 27.1 us -> 7.23 us  [the longest x1 6.32 us: body(): left = lax.ppermute(slab, 'gz', [(i, (i + 1) % GZ) for i in range(GZ)])]
    unnamed x18, local copies, waits for them, and re-layouts: 19.5 us -> 0.06 us
    pallas_call x0 -> x6, Pallas kernels: none -> 16.7 us  [call(): pl.pallas_call(kernel, out_shape=outs, in_specs=[scalar] * smem + [vmem]...]
    ppermute x5 -> x2, starting transfers between devices: 21.1 us -> 5.14 us  [the longest x1 3.82 us: body(): left = lax.ppermute(slab, 'gz', [(i, (i + 1) % GZ) for i in range(GZ)])]
    all_to_all x0 -> x1, blocking collectives: none -> 15.3 us  [body(): lax.all_to_all(returned.reshape(GZ, DEPTH, INNER), 'gz', split_axis=0, co...]
  transfers between devices with their start and end apart: 7 -> 3, of which waited for: 7 -> 3; matrix products, arithmetic and copies ran while one was open for 0% -> 6% of each run, Pallas kernels for 0% -> 4%
where the time goes in v1:
time: 68.1 us; the launch traced here: 67.6 us
  waiting for transfers between devices  17 us (25%)
  Pallas kernels  16.7 us (25%)
  blocking collectives  15.3 us (22%)
  starting transfers between devices  14.4 us (21%)
  local copies, waits for them, and re-layouts  2.67 us (4%)
  other arithmetic  1.35 us (2%)
    pallas_call x6, Pallas kernels, call(): pl.pallas_call(kernel, out_shape=outs, in_specs=[scalar] * smem + [vmem]...  16.7 us
    all_to_all x1, blocking collectives, body(): lax.all_to_all(returned.reshape(GZ, DEPTH, INNER), 'gz', split_axis=0, co...  15.3 us
    all_to_all x1, waiting for transfers between devices, body(): lax.all_to_all(spectrum, 'gz', split_axis=0, concat_axis=0, tiled=True)  9.77 us
    all_to_all x1, starting transfers between devices, body(): lax.all_to_all(spectrum, 'gz', split_axis=0, concat_axis=0, tiled=True)  9.31 us
    ppermute x1, waiting for transfers between devices, body(): left = lax.ppermute(slab, 'gz', [(i, (i + 1) % GZ) for i in range(GZ)])  6.32 us
    ppermute x1, starting transfers between devices, body(): left = lax.ppermute(slab, 'gz', [(i, (i + 1) % GZ) for i in range(GZ)])  3.82 us
    transpose x2, local copies, waits for them, and re-layouts, body(): flat = lambda w: w.transpose(4, 2, 3, 0, 1).reshape(27 * CH, CH)  1.84 us
  transfers between devices with their start and end apart: 3, of which 3 were waited for; matrix products, arithmetic and copies ran while one was open for 6% of the time, Pallas kernels for 4%

profile of v1, /device:TPU:1, one launch (start us, length us, event | category | flops | bytes accessed | tf_op | source)
XLA Modules:
  0.0 67.6 jit_solution(12568439657691840950)
XLA Ops:
  0.0 3.8 %collective-permute-start = (f32[4,4,2048]{2,1,0:T(4,128)}, f32[4,4,2048]{2,1,0:T(4,128)S(1)}, u32[]{:S(2)}, u32[]{:S(2)}) collective-permute-start(f32[4,4,2048]{2,1,0:T(4,128)} %bitcast.25), channel_id=1, source_target_pairs={{0,1},{1,2},{2,3},{3,4},{4,5},{5,6},{6,7},{7,8},{8,9},{9,10},{10,1... | collective-permute-start | bytes 393224 | tf_op jit(solution)/shard_map/ppermute | solution.py:335
  3.8 0.7 multiply_bitcast_fusion.2
  4.5 0.7 multiply_bitcast_fusion
  5.2 0.7 stack.23
  5.8 0.1 copy.17
  5.9 0.0 copy-start.8
  5.9 0.9 %copy.18 = bf16[3,3,3,16,16]{4,3,2,1,0:T(8,128)(2,1)S(1)} copy(bf16[3,3,3,16,16]{4,3,0,2,1:T(8,128)(2,1)} %bitcast.27) | data formatting | bytes 27648 | tf_op jit(solution)/shard_map/transpose | solution.py:339
  6.9 0.9 %copy.19 = bf16[3,3,3,16,16]{4,3,2,1,0:T(8,128)(2,1)S(1)} copy(bf16[3,3,3,16,16]{4,3,0,2,1:T(8,128)(2,1)} %bitcast.28) | data formatting | bytes 27648 | tf_op jit(solution)/shard_map/transpose | solution.py:339
  7.8 1.4 %shard_map.154 = (bf16[128,768]{1,0:T(8,128)(2,1)S(1)}, bf16[128,768]{1,0:T(8,128)(2,1)S(1)}, bf16[128,768]{1,0:T(8,128)(2,1)S(1)}, bf16[128,768]{1,0:T(8,128)(2,1)S(1)}) custom-call(s32[1]{0:T(128)} %bitcast.7.edge_ref, bf16[432,16]{1,0:T(8,128)(2,1)S(1)} %bitcast.22, bf16[432,16]{1,0:T(8,128)(2,1)S(1)} %bitcast.23), custom_call_target="tpu_custom_call" | custom-call | flops 1000000000 | bytes 27652 | tf_op jit(solution)/shard_map/pallas_call | solution.py:305
  9.2 6.3 %collective-permute-done.left_ref = f32[4,4,2048]{2,1,0:T(4,128)S(1)} collective-permute-done((f32[4,4,2048]{2,1,0:T(4,128)}, f32[4,4,2048]{2,1,0:T(4,128)S(1)}, u32[]{:S(2)}, u32[]{:S(2)}) %collective-permute-start) | collective-permute-done | bytes 131104 | tf_op jit(solution)/shard_map/ppermute | solution.py:335
  15.5 0.0 copy-done.8
  15.5 0.0 copy-start.3
  15.5 0.0 copy-start.5
  15.6 0.0 copy-start.6
  15.6 0.0 copy-start.7
  15.6 11.6 %shard_map.155.own_ref = bf16[16,2048]{1,0:T(8,128)(2,1)S(1)} custom-call(f32[4,4,2048]{2,1,0:T(4,128)S(1)} %collective-permute-done.left_ref, f32[4,4,2048]{2,1,0:T(4,128)S(1)} %bitcast.26, f32[64,5]{1,0:T(8,128)S(1)} %bitcast.24, bf16[128,768]{1,0:T(8,128)(2,1)S(1)} %get-tuple-element.11.w1_ref, bf16[128,768]{1,0:T(8,128)(2,1)S(1)} %get-tuple-element.12.w1m_ref, ...), custom_call_target="tpu_custom_call" | custom-call | flops 10000000000 | bytes 1049856 | tf_op jit(solution)/shard_map/pallas_call | solution.py:305
  27.2 0.0 copy-start
  27.2 0.0 copy-start.1
  27.2 1.3 %collective-permute-start.1 = (bf16[16,2048]{1,0:T(8,128)(2,1)S(1)}, bf16[16,2048]{1,0:T(8,128)(2,1)S(1)}, u32[]{:S(2)}, u32[]{:S(2)}) collective-permute-start(bf16[16,2048]{1,0:T(8,128)(2,1)S(1)} %shard_map.155.own_ref), channel_id=1, source_target_pairs={{0,64},{64,0},{128,192},{192,128},{1,65},{65,1},{129,193},{193,129... | collective-permute-start | bytes 196616 | tf_op jit(solution)/shard_map/ppermute | solution.py:358
  28.6 0.9 %collective-permute-done.1.other_ref = bf16[16,2048]{1,0:T(8,128)(2,1)S(1)} collective-permute-done((bf16[16,2048]{1,0:T(8,128)(2,1)S(1)}, bf16[16,2048]{1,0:T(8,128)(2,1)S(1)}, u32[]{:S(2)}, u32[]{:S(2)}) %collective-permute-start.1) | collective-permute-done | bytes 65568 | tf_op jit(solution)/shard_map/ppermute | solution.py:358
  29.5 0.0 copy-done.3
  29.5 0.0 copy-done.5
  29.5 0.0 copy-done.6
  29.5 0.8 %shard_map.156 = bf16[64,4,128]{2,1,0:T(4,128)(2,1)} custom-call(bf16[16,2048]{1,0:T(8,128)(2,1)S(1)} %shard_map.155.own_ref, bf16[16,2048]{1,0:T(8,128)(2,1)S(1)} %collective-permute-done.1.other_ref, bf16[256,256]{1,0:T(8,128)(2,1)S(1)} %copy-done.3, bf16[128,256]{1,0:T(8,128)(2,1)S(1)} %copy-done.5, f32[16,128]{1,0:T(8,128)S(1)} %copy-done.6), custom_call_target="tpu_custom_call" | custom-call | flops 10000000 | bytes 335872 | tf_op jit(solution)/shard_map/pallas_call | solution.py:305
  30.3 9.3 %all-to-all-start = ((bf16[64,4,128]{2,1,0:T(4,128)(2,1)}), bf16[64,4,128]{2,1,0:T(4,128)(2,1)S(1)}, u32[]{:S(2)}, u32[]{:S(2)}) async-start(bf16[64,4,128]{2,1,0:T(4,128)(2,1)} %shard_map.156), calls=%async_computation | async-start | bytes 131072 | tf_op jit(solution)/shard_map/all_to_all | solution.py:362
  39.6 0.0 copy-done.7
  39.7 0.0 copy-start.2
  39.7 0.0 copy-start.4
  39.7 1.2 %shard_map.157 = (f32[256,128]{1,0:T(8,128)S(1)}, f32[256,128]{1,0:T(8,128)S(1)}) custom-call(s32[1]{0:T(128)} %bitcast.13.at_ref, f32[256,2048]{1,0:T(8,128)S(1)} %copy-done.7), custom_call_target="tpu_custom_call" | custom-call | flops 1000000000 | bytes 2097156 | tf_op jit(solution)/shard_map/pallas_call | solution.py:305
  40.9 9.8 %all-to-all-done = bf16[64,4,128]{2,1,0:T(4,128)(2,1)S(1)} async-done(((bf16[64,4,128]{2,1,0:T(4,128)(2,1)}), bf16[64,4,128]{2,1,0:T(4,128)(2,1)S(1)}, u32[]{:S(2)}, u32[]{:S(2)}) %all-to-all-start) | async-done | bytes 65568 | tf_op jit(solution)/shard_map/all_to_all | solution.py:362
  50.6 0.0 copy-done
  50.6 0.0 copy-done.1
  50.6 0.7 shard_map.158
  51.3 15.3 %all_to_all.10.in_ref = bf16[64,4,128]{2,1,0:T(4,128)(2,1)S(1)} all-to-all(bf16[64,4,128]{2,1,0:T(4,128)(2,1)S(1)} %bitcast.21), channel_id=1, replica_groups=mesh['half'=4,'gz'=64] {'gz'}, dimensions={0} | all-to-all | bytes 131072 | tf_op jit(solution)/shard_map/all_to_all | solution.py:366
  66.7 0.0 copy-done.2
  66.7 0.0 copy-done.4
  66.7 0.9 %shard_map.159 = f32[4,4,2048]{2,1,0:T(4,128)} custom-call(bf16[64,4,128]{2,1,0:T(4,128)(2,1)S(1)} %all_to_all.10.in_ref, bf16[256,256]{1,0:T(8,128)(2,1)S(1)} %copy-done.2, bf16[128,256]{1,0:T(8,128)(2,1)S(1)} %copy-done.4, f32[16,128]{1,0:T(8,128)S(1)} %copy-done.6), custom_call_target="tpu_custom_call" | custom-call | flops 10000000 | bytes 270336 | tf_op jit(solution)/shard_map/pallas_call | solution.py:305
  (1 shorter events, 0.0 us)
Async XLA Ops:
  0.0 15.5 %collective-permute-start = (f32[4,4,2048]{2,1,0:T(4,128)}, f32[4,4,2048]{2,1,0:T(4,128)S(1)}, u32[]{:S(2)}, u32[]{:S(2)}) collective-permute-start(f32[4,4,2048]{2,1,0:T(4,128)} %bitcast.25), channel_id=1, source_target_pairs={{0,1},{1,2},{2,3},{3,4},{4,5},{5,6},{6,7},{7,8},{8,9},{9,10},{10,1... | collective-permute-start | bytes 393224 | tf_op jit(solution)/shard_map/ppermute | solution.py:335
  5.9 9.6 %copy-start.8 = (f32[1,4,4,2048]{3,2,1,0:T(4,128)S(1)}, f32[1,4,4,2048]{3,2,1,0:T(4,128)}, u32[]{:S(2)}) copy-start(f32[1,4,4,2048]{3,2,1,0:T(4,128)} %param.16) | copy-start | bytes 393220
  15.5 13.9 %copy-start.3 = (bf16[256,256]{1,0:T(8,128)(2,1)S(1)}, bf16[256,256]{1,0:T(8,128)(2,1)}, u32[]{:S(2)}) copy-start(bf16[256,256]{1,0:T(8,128)(2,1)} %constant.34.clone.full_ref) | copy-start | bytes 393220
  15.5 13.9 %copy-start.5 = (bf16[128,256]{1,0:T(8,128)(2,1)S(1)}, bf16[128,256]{1,0:T(8,128)(2,1)}, u32[]{:S(2)}) copy-start(bf16[128,256]{1,0:T(8,128)(2,1)} %constant.35.clone.ends_ref) | copy-start | bytes 196612
  15.6 13.9 %copy-start.6 = (f32[16,128]{1,0:T(8,128)S(1)}, f32[16,128]{1,0:T(8,128)}, u32[]{:S(2)}) copy-start(f32[16,128]{1,0:T(8,128)} %constant.36.clone.twiddle_ref) | copy-start | bytes 24580
  15.6 24.1 %copy-start.7 = (f32[256,2048]{1,0:T(8,128)S(1)}, f32[256,2048]{1,0:T(8,128)}, u32[]{:S(2)}) copy-start(f32[256,2048]{1,0:T(8,128)} %wedge_ref.1) | copy-start | bytes 6291460
  27.2 23.4 %copy-start = (bf16[512,256]{1,0:T(8,128)(2,1)S(1)}, bf16[512,256]{1,0:T(8,128)(2,1)}, u32[]{:S(2)}) copy-start(bf16[512,256]{1,0:T(8,128)(2,1)} %constant.37.clone.ahead_ref) | copy-start | bytes 786436
  27.2 23.4 %copy-start.1 = (bf16[512,256]{1,0:T(8,128)(2,1)S(1)}, bf16[512,256]{1,0:T(8,128)(2,1)}, u32[]{:S(2)}) copy-start(bf16[512,256]{1,0:T(8,128)(2,1)} %constant.38.clone.back_ref) | copy-start | bytes 786436
  27.2 2.2 %collective-permute-start.1 = (bf16[16,2048]{1,0:T(8,128)(2,1)S(1)}, bf16[16,2048]{1,0:T(8,128)(2,1)S(1)}, u32[]{:S(2)}, u32[]{:S(2)}) collective-permute-start(bf16[16,2048]{1,0:T(8,128)(2,1)S(1)} %shard_map.155.own_ref), channel_id=1, source_target_pairs={{0,64},{64,0},{128,192},{192,128},{1,65},{65,1},{129,193},{193,129... | collective-permute-start | bytes 196616 | tf_op jit(solution)/shard_map/ppermute | solution.py:358
  30.3 20.3 %all-to-all-start = ((bf16[64,4,128]{2,1,0:T(4,128)(2,1)}), bf16[64,4,128]{2,1,0:T(4,128)(2,1)S(1)}, u32[]{:S(2)}, u32[]{:S(2)}) async-start(bf16[64,4,128]{2,1,0:T(4,128)(2,1)} %shard_map.156), calls=%async_computation | async-start | bytes 131072 | tf_op jit(solution)/shard_map/all_to_all | solution.py:362
  39.7 27.0 %copy-start.2 = (bf16[256,256]{1,0:T(8,128)(2,1)S(1)}, bf16[256,256]{1,0:T(8,128)(2,1)}, u32[]{:S(2)}) copy-start(bf16[256,256]{1,0:T(8,128)(2,1)} %constant.39.clone.full_ref) | copy-start | bytes 393220
  39.7 27.0 %copy-start.4 = (bf16[128,256]{1,0:T(8,128)(2,1)S(1)}, bf16[128,256]{1,0:T(8,128)(2,1)}, u32[]{:S(2)}) copy-start(bf16[128,256]{1,0:T(8,128)(2,1)} %constant.40.clone.ends_ref) | copy-start | bytes 196612

commit v2 on v1

--- a/solution.py
+++ b/solution.py
@@ -63,15 +63,11 @@
     return ahead.astype(jnp.bfloat16), back.astype(jnp.bfloat16)
 
 
-def weights_kernel(edge_ref, first_ref, second_ref, w1_ref, w1m_ref, w2a_ref, w2b_ref):
+def build_weights(inner, conv, outs):
     rows = lax.broadcasted_iota(jnp.int32, (128, 256), 0)
     cols = lax.broadcasted_iota(jnp.int32, (128, 256), 1)
     zo, yo = rows // 64, rows % 4
     zi, yi = cols // 64, cols % 4
-    inner = edge_ref[0] == 0
-    keep_mid = ((zi >= 2) == (zo == 1)) | inner
-    keep_low = (zi <= 2) | inner
-    keep_high = (zi >= 1) | inner
     spread_rows = (
         lax.broadcasted_iota(jnp.int32, (128, CH), 0) % 64 // 4
         == lax.broadcasted_iota(jnp.int32, (128, CH), 1)
@@ -83,92 +79,129 @@
     place = (zi - zo) * 3 + (yi - yo + 1)
     valid = (yi - yo + 1 >= 0) & (yi - yo + 1 <= 2) & (zi - zo >= 0) & (zi - zo <= 2)
     place = jnp.where(valid, place, -1)
-    for src, outs in (
-        (first_ref, ((w1_ref, None), (w1m_ref, keep_mid))),
-        (second_ref, ((w2a_ref, keep_low), (w2b_ref, keep_high))),
-    ):
-        wide = dot(src[...], spread_cols).astype(BF16)
-        for e in range(3):
-            total = jnp.zeros((128, 256), F32)
-            for ab in range(9):
-                at = (e * 9 + ab) * CH
-                total = jnp.where(place == ab, dot(spread_rows, wide[at : at + CH]), total)
-            total = total * 0.5
-            for out, keep in outs:
-                part = total if keep is None else jnp.where(keep, total, 0.0)
-                out[:, e * 256 : (e + 1) * 256] = part.astype(BF16)
+    keeps = {
+        "all": None,
+        "middle": ((zi >= 2) == (zo == 1)) | inner,
+        "low": (zi <= 2) | inner,
+        "high": (zi >= 1) | inner,
+    }
+    wide = dot(conv, spread_cols).astype(BF16)
+    for e in range(3):
+        total = jnp.zeros((128, 256), F32)
+        for ab in range(9):
+            at = (ab * 3 + e) * CH
+            total = jnp.where(place == ab, dot(spread_rows, wide[at : at + CH]), total)
+        total = total * 0.5
+        for out, name in outs:
+            part = total if keeps[name] is None else jnp.where(keeps[name], total, 0.0)
+            out[:, e * 256 : (e + 1) * 256] = part.astype(BF16)
 
 
 def silu_of_half(h):
     return h + h * jnp.tanh(h)
 
 
+def across(column, width):
+    return jnp.concatenate([column] * (width // INNER), axis=1)
+
+
+def shifts(ref, row, value):
+    lane = lax.broadcasted_iota(jnp.int32, (16, NX), 1)
+    none = jnp.zeros_like(value)
+    ref[0, row : row + 16, :] = jnp.where(lane == 0, none, pltpu.roll(value, 1, 1))
+    ref[2, row : row + 16, :] = jnp.where(lane == NX - 1, none, pltpu.roll(value, NX - 1, 1))
+
+
+def lift(slab_ref, x_ref, par_ref):
+    for z in range(DEPTH):
+        cells = jnp.concatenate([slab_ref[z]] * 4, axis=0)
+        for block in range(4):
+            rows = slice(block * 16, block * 16 + 16)
+            value = silu_of_half(across(par_ref[0, rows], NX) * cells + across(par_ref[1, rows], NX))
+            value = value.astype(BF16)
+            x_ref[1, z * 64 + block * 16 : z * 64 + block * 16 + 16, :] = value
+            shifts(x_ref, z * 64 + block * 16, value)
+
+
+def shift_rows(x_ref, first, count):
+    for block in range(count):
+        row = first + block * 16
+        shifts(x_ref, row, x_ref[1, row : row + 16, :])
+
+
+CHUNK = 256
+
+
+def convolve(w_ref, parts, bias, at):
+    total = bias
+    for e in range(3):
+        cells = [ref[e, row : row + size, at : at + CHUNK] for ref, row, size in parts]
+        cells = cells[0] if len(cells) == 1 else jnp.concatenate(cells, 0)
+        total = total + dot(w_ref[:, e * 256 : (e + 1) * 256], cells)
+    return silu_of_half(total)
+
+
+def bias_of(par_ref, index):
+    return across(jnp.concatenate([par_ref[index]] * 2, 0), CHUNK)
+
+
+def prepare_kernel(
+    at_ref, slab_ref, small_ref, par_ref, w1_ref, w1m_ref, w2a_ref, w2b_ref, x1_ref, x2_ref
+):
+    channel = lax.broadcasted_iota(jnp.int32, (4 * CH, CH), 0) // 4
+    mine = channel == lax.broadcasted_iota(jnp.int32, (4 * CH, CH), 1)
+    for index in range(5):
+        values = small_ref[2 * 27 * CH + index : 2 * 27 * CH + index + 1, :]
+        column = jnp.sum(jnp.where(mine, values, 0.0), axis=1, keepdims=True)
+        if index < 4:
+            column = 0.5 * column
+        par_ref[index] = jnp.broadcast_to(column, (4 * CH, INNER))
+    first = small_ref[: 27 * CH].astype(BF16)
+    second = small_ref[27 * CH : 2 * 27 * CH].astype(BF16)
+    inner = at_ref[0] > 0
+    build_weights(inner, first, ((w1_ref, "all"), (w1m_ref, "middle")))
+    build_weights(inner, second, ((w2a_ref, "low"), (w2b_ref, "high")))
+    lift(slab_ref, x1_ref, par_ref)
+    bias = bias_of(par_ref, 2)
+    for at in range(0, NX, CHUNK):
+        act = convolve(w1_ref, ((x1_ref, 0, 256),), bias, at)
+        x2_ref[1, :, at : at + CHUNK] = act.astype(BF16)
+    shift_rows(x2_ref, 0, 8)
+
+
 def filter_kernel(
-    left_ref, own_ref, par_ref, w1_ref, w1m_ref, w2a_ref, w2b_ref, out_ref, x1, x2
+    left_ref, own_ref, par_ref, w1_ref, w1m_ref, w2a_ref, w2b_ref, x1_ref, x2_ref,
+    full_ref, ends_ref, twiddle_ref, out_ref, x1, x2,
 ):
-    lane = lax.broadcasted_iota(jnp.int32, (16, NX), 1)
-    at_start, at_end = lane == 0, lane == NX - 1
-
-    def spread(ref, row, value):
-        rows = pl.ds(row, 16)
-        wide = value.astype(F32)
-        ref[1, rows, :] = value
-        ref[0, rows, :] = jnp.where(at_start, 0.0, pltpu.roll(wide, 1, 1)).astype(BF16)
-        ref[2, rows, :] = jnp.where(at_end, 0.0, pltpu.roll(wide, NX - 1, 1)).astype(BF16)
-
-    for z in range(2 * DEPTH):
-        cells = left_ref[z] if z < DEPTH else own_ref[z - DEPTH]
-        cells = jnp.concatenate([cells] * 4, axis=0)
-        for block in range(4):
-            gain = par_ref[block * 16 : block * 16 + 16, 0:1]
-            shift = par_ref[block * 16 : block * 16 + 16, 1:2]
-            lifted = silu_of_half(gain * cells + shift).astype(BF16)
-            spread(x1, z * 64 + block * 16, lifted)
-
-    chunk = 256
-
-    def three(w_ref, x_ref, row, at):
-        total = None
-        for e in range(3):
-            part = dot(w_ref[:, e * 256 : (e + 1) * 256], x_ref[e, row : row + 256, pl.ds(at, chunk)])
-            total = part if total is None else total + part
-        return total
-
-    bias1 = par_ref[:, 2:3]
-    bias1 = jnp.concatenate([bias1, bias1], 0)
-
-    @pl.loop(0, NX // chunk)
-    def _(index):
-        at = pl.multiple_of(index * chunk, chunk)
-        for g, w_ref in enumerate((w1_ref, w1m_ref, w1_ref)):
-            pre = three(w_ref, x1, 128 * g, at) + bias1
-            x2[1, 128 * g : 128 * g + 128, pl.ds(at, chunk)] = silu_of_half(pre).astype(BF16)
-
-    @pl.loop(0, 24)
-    def _(index):
-        row = pl.multiple_of(index * 16, 16)
-        spread(x2, row, x2[1, pl.ds(row, 16), :])
-
-    bias2 = par_ref[:, 3:4]
-    bias2 = jnp.concatenate([bias2, bias2], 0)
-    mix = par_ref[:, 4:5]
-
-    @pl.loop(0, NX // chunk)
-    def _(index):
-        at = pl.multiple_of(index * chunk, chunk)
+    lift(left_ref, x1, par_ref)
+    bias = bias_of(par_ref, 2)
+    for at in range(0, NX, CHUNK):
+        act = convolve(w1_ref, ((x1, 0, 256),), bias, at)
+        x2[1, :128, at : at + CHUNK] = act.astype(BF16)
+        act = convolve(w1m_ref, ((x1, 128, 128), (x1_ref, 0, 128)), bias, at)
+        x2[1, 128:, at : at + CHUNK] = act.astype(BF16)
+    shift_rows(x2, 0, 16)
+    bias = bias_of(par_ref, 3)
+    mix = across(par_ref[4], CHUNK)
+    a = []
+    for at in range(0, NX, CHUNK):
         slices = []
-        for g, w_ref in enumerate((w2a_ref, w2b_ref)):
-            act = silu_of_half(three(w_ref, x2, 128 * g, at) + bias2)
+        for w_ref, parts in (
+            (w2a_ref, ((x2, 0, 256),)),
+            (w2b_ref, ((x2, 128, 128), (x2_ref, 0, 128))),
+        ):
+            act = convolve(w_ref, parts, bias, at)
             for zo in range(2):
                 terms = act[zo * 64 : zo * 64 + 64] * mix
                 total = terms[0:8]
                 for pair in range(1, 8):
                     total = total + terms[pair * 8 : pair * 8 + 8]
-                z = 2 + 2 * g + zo
-                base = left_ref[z, :, pl.ds(at, chunk)] if z < DEPTH else own_ref[z - DEPTH, :, pl.ds(at, chunk)]
+                z = 2 + len(slices)
+                base = left_ref[z, :, at : at + CHUNK] if z < DEPTH else own_ref[z - DEPTH, :, at : at + CHUNK]
                 slices.append(base + total[0:4] + total[4:8])
         mixed = jnp.concatenate([slices[z][y : y + 1] for y in range(NY) for z in range(DEPTH)], 0)
-        out_ref[:, pl.ds(at, chunk)] = mixed.astype(BF16)
+        a += [mixed[:, i : i + INNER] for i in range(0, CHUNK, INNER)]
+    forward(a, full_ref, ends_ref, twiddle_ref, out_ref)
 
 
 def cos16(n):
@@ -194,9 +227,7 @@
     return total
 
 
-def forward_kernel(own_ref, other_ref, full_ref, ends_ref, twiddle_ref, out_ref):
-    delta = own_ref[...].astype(F32) - other_ref[...].astype(F32)
-    a = [delta[:, INNER * i : INNER * (i + 1)] for i in range(RADIX)]
+def forward(a, full_ref, ends_ref, twiddle_ref, out_ref):
     plus = [a[i] + a[16 - i] for i in range(1, 8)]
     minus = [a[i] - a[16 - i] for i in range(1, 8)]
     re, im = [], []
@@ -255,7 +286,7 @@
 
 
 def wedge_kernel(at_ref, wedge_ref, plus_ref, minus_ref):
-    block = at_ref[0]
+    block = at_ref[0] % BLOCKS
     k = lax.broadcasted_iota(jnp.int32, (NX, INNER), 0)
     j = lax.broadcasted_iota(jnp.int32, (NX, INNER), 1)
     col = j % HALF
@@ -286,9 +317,10 @@
         out[...] = both
 
 
-def middle_kernel(in_ref, plus_ref, minus_ref, ahead_ref, back_ref, out_ref):
+def middle_kernel(own_ref, other_ref, plus_ref, minus_ref, ahead_ref, back_ref, out_ref):
+    delta = (own_ref[...].astype(F32) - other_ref[...].astype(F32)).astype(BF16)
     sign = jnp.where(lax.broadcasted_iota(jnp.int32, (NZ, INNER), 1) < HALF, 1.0, -1.0)
-    both = dot(ahead_ref[...], in_ref[...])
+    both = dot(ahead_ref[...], delta)
     cos_part, sin_part = both[:NZ], pltpu.roll(both[NZ:], HALF, 1)
     freq = cos_part + sign * sin_part
     mirror = sign * cos_part - sin_part
@@ -299,14 +331,13 @@
 
 def call(kernel, outs, *args, scratch=(), megabytes=8, smem=0, flops=10**7):
     many = isinstance(outs, list)
-    vmem = pl.BlockSpec(memory_space=pltpu.VMEM)
-    scalar = pl.BlockSpec(memory_space=pltpu.SMEM)
+    spec = lambda space: pl.BlockSpec(memory_space=space)
     moved = sum(a.size * a.dtype.itemsize for a in args)
     return pl.pallas_call(
         kernel,
         out_shape=outs,
-        in_specs=[scalar] * smem + [vmem] * (len(args) - smem),
-        out_specs=[vmem] * len(outs) if many else vmem,
+        in_specs=[spec(pltpu.SMEM)] * smem + [spec(pltpu.VMEM)] * (len(args) - smem),
+        out_specs=[spec(pltpu.VMEM)] * len(outs) if many else spec(pltpu.VMEM),
         scratch_shapes=scratch,
         compiler_params=params(megabytes),
         cost_estimate=pl.CostEstimate(flops=flops, bytes_accessed=moved, transcendentals=0),
@@ -334,34 +365,29 @@
     slab = density[0]
     left = lax.ppermute(slab, "gz", [(i, (i + 1) % GZ) for i in range(GZ)])
 
-    edge = (place == 0).astype(jnp.int32).reshape(1)
-    block = (place % BLOCKS).astype(jnp.int32).reshape(1)
-    flat = lambda w: w.transpose(4, 2, 3, 0, 1).reshape(27 * CH, CH)
-    weights = call(
-        weights_kernel, [shape(128, 768)] * 4, edge, flat(conv_first), flat(conv_second),
-        smem=1, megabytes=16, flops=10**9,
+    flat = lambda w: w.transpose(2, 3, 4, 0, 1).reshape(27 * CH, CH)
+    at = place.astype(jnp.int32).reshape(1)
+    vectors = jnp.stack([lift_weight, lift_bias, bias_first, bias_second, projection])
+    small = jnp.concatenate([flat(conv_first).astype(F32), flat(conv_second).astype(F32), vectors], 0)
+    par, w1, w1m, w2a, w2b, x1, x2 = call(
+        prepare_kernel,
+        [shape(5, 4 * CH, INNER, dtype=F32)] + [shape(128, 768)] * 4 + [shape(3, 256, NX), shape(3, 128, NX)],
+        at, slab, small, smem=1, megabytes=24, flops=10**9,
     )
     plus, minus = call(
-        wedge_kernel, [shape(NZ, INNER, dtype=F32)] * 2, block, wedge,
-        smem=1, megabytes=32, flops=10**9,
-    )
-    columns = jnp.stack(
-        [0.5 * lift_weight, 0.5 * lift_bias, 0.5 * bias_first, 0.5 * bias_second, projection], 1
-    )
-    columns = jnp.repeat(columns, NY, axis=0)
-
-    mixed = call(
-        filter_kernel, shape(NY * DEPTH, NX), left, slab, columns, *weights,
-        scratch=[pltpu.VMEM((3, 512, NX), BF16), pltpu.VMEM((3, 384, NX), BF16)],
-        megabytes=40, flops=10**10,
-    )
-    other = lax.ppermute(mixed, "half", [(i, i ^ 1) for i in range(lax.axis_size("half"))])
+        wedge_kernel, [shape(NZ, INNER, dtype=F32)] * 2, at, wedge, smem=1, megabytes=16, flops=10**9,
+    )
     spectrum = call(
-        forward_kernel, shape(GZ, DEPTH, INNER), mixed, other, full_x, ends_x, twiddle,
+        filter_kernel, shape(GZ, DEPTH, INNER), left, slab, par, w1, w1m, w2a, w2b, x1, x2,
+        full_x, ends_x, twiddle,
+        scratch=[pltpu.VMEM((3, 256, NX), BF16), pltpu.VMEM((3, 256, NX), BF16)],
+        megabytes=24, flops=10**9,
     )
     pencils = lax.all_to_all(spectrum, "gz", split_axis=0, concat_axis=0, tiled=True)
+    pencils = pencils.reshape(NZ, INNER)
+    other = lax.ppermute(pencils, "half", [(i, i ^ 1) for i in range(lax.axis_size("half"))])
     returned = call(
-        middle_kernel, shape(NZ, INNER), pencils.reshape(NZ, INNER), plus, minus, ahead, back,
+        middle_kernel, shape(NZ, INNER), pencils, other, plus, minus, ahead, back,
     )
     slabs = lax.all_to_all(
         returned.reshape(GZ, DEPTH, INNER), "gz", split_axis=0, concat_axis=0, tiled=True

time: 68.1 us -> 59.3 us (0.87)
  blocking collectives: 15.3 us -> 35.4 us
  waiting for transfers between devices: 17 us -> 5.72 us
  Pallas kernels: 16.7 us -> 8 us
  starting transfers between devices: 14.4 us -> 6.22 us
  local copies, waits for them, and re-layouts: 2.67 us -> 1.76 us
    all_to_all x0 -> x1, blocking collectives: none -> 20.5 us  [body(): lax.all_to_all(spectrum, 'gz', split_axis=0, concat_axis=0, tiled=True)]
    all_to_all x1 -> x0, waiting for transfers between devices: 9.77 us -> none  [body(): lax.all_to_all(spectrum, 'gz', split_axis=0, concat_axis=0, tiled=True)]
    all_to_all x1 -> x0, starting transfers between devices: 9.31 us -> none  [body(): lax.all_to_all(spectrum, 'gz', split_axis=0, concat_axis=0, tiled=True)]
    pallas_call x6 -> x5, Pallas kernels: 16.7 us -> 8 us  [call(): pl.pallas_call(kernel, out_shape=outs, in_specs=[spec(pltpu.SMEM)] * smem...]
    transpose x2 -> x0, local copies, waits for them, and re-layouts: 1.84 us -> none  [body(): flat = lambda w: w.transpose(4, 2, 3, 0, 1).reshape(27 * CH, CH)]
    convert_element_type x0 -> x2, other arithmetic: none -> 1.83 us  [the longest x1 0.92 us: body(): flat(conv_second).astype(F32)]
    another operation x2 -> x0, other arithmetic: 1.35 us -> none  [body(): jnp.stack([0.5 * lift_weight, 0.5 * lift_bias, 0.5 * bias_first, 0.5 * bi...]
    ppermute x1, starting transfers between devices: 1.32 us -> 2.4 us  [body(): lax.ppermute(pencils, 'half', [(i, i ^ 1) for i in range(lax.axis_size('h...]
  transfers between devices with their start and end apart: 3 -> 2, of which waited for: 3 -> 1; matrix products, arithmetic and copies ran while one was open for 6% -> 4% of each run, Pallas kernels for 4% -> 6%
where the time goes in v2:
time: 59.3 us; the launch traced here: 59 us
  blocking collectives  35.4 us (60%)
  Pallas kernels  8 us (13%)
  starting transfers between devices  6.22 us (10%)
  waiting for transfers between devices  5.72 us (10%)
  other arithmetic  1.83 us (3%)
  local copies, waits for them, and re-layouts  1.76 us (3%)
    all_to_all x1, blocking collectives, body(): lax.all_to_all(spectrum, 'gz', split_axis=0, concat_axis=0, tiled=True)  20.5 us
    all_to_all x1, blocking collectives, body(): lax.all_to_all(returned.reshape(GZ, DEPTH, INNER), 'gz', split_axis=0, co...  14.9 us
    pallas_call x5, Pallas kernels, call(): pl.pallas_call(kernel, out_shape=outs, in_specs=[spec(pltpu.SMEM)] * smem...  8 us
    ppermute x1, waiting for transfers between devices, body(): left = lax.ppermute(slab, 'gz', [(i, (i + 1) % GZ) for i in range(GZ)])  5.71 us
    ppermute x1, starting transfers between devices, body(): left = lax.ppermute(slab, 'gz', [(i, (i + 1) % GZ) for i in range(GZ)])  3.82 us
    ppermute x1, starting transfers between devices, body(): lax.ppermute(pencils, 'half', [(i, i ^ 1) for i in range(lax.axis_size('h...  2.4 us
  transfers between devices with their start and end apart: 2, of which 1 were waited for; matrix products, arithmetic and copies ran while one was open for 4% of the time, Pallas kernels for 6%

profile of v2, /device:TPU:1, one launch (start us, length us, event | category | flops | bytes accessed | tf_op | source)
XLA Modules:
  0.0 59.0 jit_solution(14712010099856105133)
XLA Ops:
  0.0 3.8 %collective-permute-start = (f32[4,4,2048]{2,1,0:T(4,128)}, f32[4,4,2048]{2,1,0:T(4,128)S(1)}, u32[]{:S(2)}, u32[]{:S(2)}) collective-permute-start(f32[4,4,2048]{2,1,0:T(4,128)} %bitcast.19), channel_id=1, source_target_pairs={{0,1},{1,2},{2,3},{3,4},{4,5},{5,6},{6,7},{7,8},{8,9},{9,10},{10,1... | collective-permute-start | bytes 393224 | tf_op jit(solution)/shard_map/ppermute | solution.py:366
  3.8 0.9 %convert_element_type.26 = f32[16,16,3,3,3]{1,0,4,3,2:T(8,128)S(1)} convert(bf16[16,16,3,3,3]{1,0,4,3,2:T(8,128)(2,1)} %param.19) | non-fusion elementwise | flops 6912 | bytes 41472 | tf_op jit(solution)/shard_map/convert_element_type | solution.py:371
  4.7 0.9 %convert_element_type.27 = f32[16,16,3,3,3]{1,0,4,3,2:T(8,128)S(1)} convert(bf16[16,16,3,3,3]{1,0,4,3,2:T(8,128)(2,1)} %param.21) | non-fusion elementwise | flops 6912 | bytes 41472 | tf_op jit(solution)/shard_map/convert_element_type | solution.py:371
  5.7 0.0 copy-start.4
  5.7 0.0 copy-start.5
  5.7 0.0 copy-start.7
  5.7 0.8 %concatenate.3.small_ref = f32[869,16]{1,0:T(8,128)S(1)} concatenate(f32[432,16]{1,0:T(8,128)S(1)} %bitcast.22, f32[432,16]{1,0:T(8,128)S(1)} %bitcast.23, f32[1,16]{1,0:T(1,128)} %bitcast.24, f32[1,16]{1,0:T(1,128)} %bitcast.25, f32[1,16]{1,0:T(1,128)} %bitcast.26, f32[1,16]{1,0:T(1,128)} %bitcast.27, f32[1,16]{1,0:T(1,128)} %bitcast.28), dimensions={0} | concatenate | bytes 111232 | tf_op jit(solution)/shard_map/concatenate | solution.py:371
  6.5 0.0 copy-start.2
  6.5 0.9 %copy-done.2 = f32[1,4,4,2048]{3,2,1,0:T(4,128)S(1)} copy-done((f32[1,4,4,2048]{3,2,1,0:T(4,128)S(1)}, f32[1,4,4,2048]{3,2,1,0:T(4,128)}, u32[]{:S(2)}) %copy-start.2) | copy-done | bytes 131096
  7.4 2.4 %shard_map.154 = (f32[5,64,128]{2,1,0:T(8,128)S(1)}, bf16[128,768]{1,0:T(8,128)(2,1)S(1)}, bf16[128,768]{1,0:T(8,128)(2,1)S(1)}, bf16[128,768]{1,0:T(8,128)(2,1)...) custom-call(s32[1]{0:T(128)} %bitcast.1.at_ref, ...), custom_call_target="tpu_custom_call" | custom-call | flops 1000000000 | bytes 186692 | tf_op jit(solution)/shard_map/pallas_call | solution.py:336
  9.8 5.7 %collective-permute-done.left_ref = f32[4,4,2048]{2,1,0:T(4,128)S(1)} collective-permute-done((f32[4,4,2048]{2,1,0:T(4,128)}, f32[4,4,2048]{2,1,0:T(4,128)S(1)}, u32[]{:S(2)}, u32[]{:S(2)}) %collective-permute-start) | collective-permute-done | bytes 131104 | tf_op jit(solution)/shard_map/ppermute | solution.py:366
  15.5 0.0 copy-done.4
  15.5 0.0 copy-done.5
  15.5 0.0 copy-done.7
  15.5 0.0 copy-start.8
  15.5 2.8 %shard_map.155 = bf16[64,4,128]{2,1,0:T(4,128)(2,1)S(1)} custom-call(f32[4,4,2048]{2,1,0:T(4,128)S(1)} %collective-permute-done.left_ref, f32[4,4,2048]{2,1,0:T(4,128)S(1)} %bitcast.21, f32[5,64,128]{2,1,0:T(8,128)S(1)} %get-tuple-element.14.par_ref, bf16[128,768]{1,0:T(8,128)(2,1)S(1)} %get-tuple-element.15.w1_ref, ...), custom_call_target="tpu_custom_call" | custom-call | flops 1000000000 | bytes 6135808 | tf_op jit(solution)/shard_map/pallas_call | solution.py:336
  18.4 0.0 copy-start
  18.4 0.0 copy-start.1
  18.4 20.5 %all_to_all.10 = bf16[64,4,128]{2,1,0:T(4,128)(2,1)S(1)} all-to-all(bf16[64,4,128]{2,1,0:T(4,128)(2,1)S(1)} %shard_map.155), channel_id=1, replica_groups=mesh['half'=4,'gz'=64] {'gz'}, dimensions={0} | all-to-all | bytes 131072 | tf_op jit(solution)/shard_map/all_to_all | solution.py:386
  38.9 0.0 copy-start.3
  38.9 0.0 copy-start.6
  38.9 2.4 %collective-permute-start.1 = (bf16[256,128]{1,0:T(8,128)(2,1)S(1)}, bf16[256,128]{1,0:T(8,128)(2,1)S(1)}, u32[]{:S(2)}, u32[]{:S(2)}) collective-permute-start(bf16[256,128]{1,0:T(8,128)(2,1)S(1)} %bitcast.16), channel_id=1, source_target_pairs={{0,64},{64,0},{128,192},{192,128},{1,65},{65,1},{129,193},{193,129... | collective-permute-start | bytes 196616 | tf_op jit(solution)/shard_map/ppermute | solution.py:388
  41.3 0.0 copy-done.8
  41.3 1.2 %shard_map.156 = (f32[256,128]{1,0:T(8,128)S(1)}, f32[256,128]{1,0:T(8,128)S(1)}) custom-call(s32[1]{0:T(128)} %bitcast.1.at_ref, f32[256,2048]{1,0:T(8,128)S(1)} %copy-done.8), custom_call_target="tpu_custom_call" | custom-call | flops 1000000000 | bytes 2097156 | tf_op jit(solution)/shard_map/pallas_call | solution.py:336
  42.5 0.0 collective-permute-done.1.other_ref
  42.5 0.0 copy-done
  42.5 0.0 copy-done.1
  42.5 0.7 %shard_map.157 = bf16[256,128]{1,0:T(8,128)(2,1)S(1)} custom-call(bf16[256,128]{1,0:T(8,128)(2,1)S(1)} %bitcast.17, bf16[256,128]{1,0:T(8,128)(2,1)S(1)} %collective-permute-done.1.other_ref, f32[256,128]{1,0:T(8,128)S(1)} %get-tuple-element.21.plus_ref, f32[256,128]{1,0:T(8,128)S(1)} %get-tuple-element.22.minus_ref, bf16[512,256]{1,0:T(8,128)(2,1)S(1)} %copy-done, ...), custom_call_target="tpu_custom_call" | custom-call | flops 10000000 | bytes 917504 | tf_op jit(solution)/shard_map/pallas_call | solution.py:336
  43.2 14.9 %all_to_all.11.in_ref = bf16[64,4,128]{2,1,0:T(4,128)(2,1)S(1)} all-to-all(bf16[64,4,128]{2,1,0:T(4,128)(2,1)S(1)} %bitcast.18), channel_id=1, replica_groups=mesh['half'=4,'gz'=64] {'gz'}, dimensions={0} | all-to-all | bytes 131072 | tf_op jit(solution)/shard_map/all_to_all | solution.py:392
  58.1 0.0 copy-done.3
  58.1 0.0 copy-done.6
  58.1 0.9 %shard_map.158 = f32[4,4,2048]{2,1,0:T(4,128)} custom-call(bf16[64,4,128]{2,1,0:T(4,128)(2,1)S(1)} %all_to_all.11.in_ref, bf16[256,256]{1,0:T(8,128)(2,1)S(1)} %copy-done.3, bf16[128,256]{1,0:T(8,128)(2,1)S(1)} %copy-done.6, f32[16,128]{1,0:T(8,128)S(1)} %copy-done.7), custom_call_target="tpu_custom_call" | custom-call | flops 10000000 | bytes 270336 | tf_op jit(solution)/shard_map/pallas_call | solution.py:336
Async XLA Ops:
  0.0 15.5 %collective-permute-start = (f32[4,4,2048]{2,1,0:T(4,128)}, f32[4,4,2048]{2,1,0:T(4,128)S(1)}, u32[]{:S(2)}, u32[]{:S(2)}) collective-permute-start(f32[4,4,2048]{2,1,0:T(4,128)} %bitcast.19), channel_id=1, source_target_pairs={{0,1},{1,2},{2,3},{3,4},{4,5},{5,6},{6,7},{7,8},{8,9},{9,10},{10,1... | collective-permute-start | bytes 393224 | tf_op jit(solution)/shard_map/ppermute | solution.py:366
  5.7 9.9 %copy-start.4 = (bf16[256,256]{1,0:T(8,128)(2,1)S(1)}, bf16[256,256]{1,0:T(8,128)(2,1)}, u32[]{:S(2)}) copy-start(bf16[256,256]{1,0:T(8,128)(2,1)} %constant.18.clone.full_ref) | copy-start | bytes 393220
  5.7 9.9 %copy-start.5 = (bf16[128,256]{1,0:T(8,128)(2,1)S(1)}, bf16[128,256]{1,0:T(8,128)(2,1)}, u32[]{:S(2)}) copy-start(bf16[128,256]{1,0:T(8,128)(2,1)} %constant.19.clone.ends_ref) | copy-start | bytes 196612
  5.7 9.8 %copy-start.7 = (f32[16,128]{1,0:T(8,128)S(1)}, f32[16,128]{1,0:T(8,128)}, u32[]{:S(2)}) copy-start(f32[16,128]{1,0:T(8,128)} %constant.20.clone.twiddle_ref) | copy-start | bytes 24580
  6.5 0.9 %copy-start.2 = (f32[1,4,4,2048]{3,2,1,0:T(4,128)S(1)}, f32[1,4,4,2048]{3,2,1,0:T(4,128)}, u32[]{:S(2)}) copy-start(f32[1,4,4,2048]{3,2,1,0:T(4,128)} %param.16) | copy-start | bytes 393220
  15.5 25.8 %copy-start.8 = (f32[256,2048]{1,0:T(8,128)S(1)}, f32[256,2048]{1,0:T(8,128)}, u32[]{:S(2)}) copy-start(f32[256,2048]{1,0:T(8,128)} %wedge_ref.1) | copy-start | bytes 6291460
  18.4 24.2 %copy-start = (bf16[512,256]{1,0:T(8,128)(2,1)S(1)}, bf16[512,256]{1,0:T(8,128)(2,1)}, u32[]{:S(2)}) copy-start(bf16[512,256]{1,0:T(8,128)(2,1)} %constant.21.clone.ahead_ref) | copy-start | bytes 786436
  18.4 24.2 %copy-start.1 = (bf16[512,256]{1,0:T(8,128)(2,1)S(1)}, bf16[512,256]{1,0:T(8,128)(2,1)}, u32[]{:S(2)}) copy-start(bf16[512,256]{1,0:T(8,128)(2,1)} %constant.22.clone.back_ref) | copy-start | bytes 786436
  38.9 19.2 %copy-start.3 = (bf16[256,256]{1,0:T(8,128)(2,1)S(1)}, bf16[256,256]{1,0:T(8,128)(2,1)}, u32[]{:S(2)}) copy-start(bf16[256,256]{1,0:T(8,128)(2,1)} %constant.23.clone.full_ref) | copy-start | bytes 393220
  38.9 19.2 %copy-start.6 = (bf16[128,256]{1,0:T(8,128)(2,1)S(1)}, bf16[128,256]{1,0:T(8,128)(2,1)}, u32[]{:S(2)}) copy-start(bf16[128,256]{1,0:T(8,128)(2,1)} %constant.24.clone.ends_ref) | copy-start | bytes 196612
  38.9 3.6 %collective-permute-start.1 = (bf16[256,128]{1,0:T(8,128)(2,1)S(1)}, bf16[256,128]{1,0:T(8,128)(2,1)S(1)}, u32[]{:S(2)}, u32[]{:S(2)}) collective-permute-start(bf16[256,128]{1,0:T(8,128)(2,1)S(1)} %bitcast.16), channel_id=1, source_target_pairs={{0,64},{64,0},{128,192},{192,128},{1,65},{65,1},{129,193},{193,129... | collective-permute-start | bytes 196616 | tf_op jit(solution)/shard_map/ppermute | solution.py:388

commit v3 on v2

--- a/solution.py
+++ b/solution.py
@@ -63,7 +63,7 @@
     return ahead.astype(jnp.bfloat16), back.astype(jnp.bfloat16)
 
 
-def build_weights(inner, conv, outs):
+def build_weights(inner, conv_ref, layer, outs):
     rows = lax.broadcasted_iota(jnp.int32, (128, 256), 0)
     cols = lax.broadcasted_iota(jnp.int32, (128, 256), 1)
     zo, yo = rows // 64, rows % 4
@@ -85,11 +85,11 @@
         "low": (zi <= 2) | inner,
         "high": (zi >= 1) | inner,
     }
-    wide = dot(conv, spread_cols).astype(BF16)
+    wide = dot(conv_ref[...], spread_cols).astype(BF16)
     for e in range(3):
         total = jnp.zeros((128, 256), F32)
         for ab in range(9):
-            at = (ab * 3 + e) * CH
+            at = ((ab * 3 + e) * 2 + layer) * CH
             total = jnp.where(place == ab, dot(spread_rows, wide[at : at + CH]), total)
         total = total * 0.5
         for out, name in outs:
@@ -114,7 +114,7 @@
 
 def lift(slab_ref, x_ref, par_ref):
     for z in range(DEPTH):
-        cells = jnp.concatenate([slab_ref[z]] * 4, axis=0)
+        cells = jnp.concatenate([slab_ref[z].astype(F32)] * 4, axis=0)
         for block in range(4):
             rows = slice(block * 16, block * 16 + 16)
             value = silu_of_half(across(par_ref[0, rows], NX) * cells + across(par_ref[1, rows], NX))
@@ -146,21 +146,19 @@
 
 
 def prepare_kernel(
-    at_ref, slab_ref, small_ref, par_ref, w1_ref, w1m_ref, w2a_ref, w2b_ref, x1_ref, x2_ref
+    at_ref, slab_ref, conv_ref, vector_ref, par_ref, w1_ref, w1m_ref, w2a_ref, w2b_ref, x1_ref, x2_ref
 ):
     channel = lax.broadcasted_iota(jnp.int32, (4 * CH, CH), 0) // 4
     mine = channel == lax.broadcasted_iota(jnp.int32, (4 * CH, CH), 1)
     for index in range(5):
-        values = small_ref[2 * 27 * CH + index : 2 * 27 * CH + index + 1, :]
+        values = vector_ref[index : index + 1, :]
         column = jnp.sum(jnp.where(mine, values, 0.0), axis=1, keepdims=True)
         if index < 4:
             column = 0.5 * column
         par_ref[index] = jnp.broadcast_to(column, (4 * CH, INNER))
-    first = small_ref[: 27 * CH].astype(BF16)
-    second = small_ref[27 * CH : 2 * 27 * CH].astype(BF16)
     inner = at_ref[0] > 0
-    build_weights(inner, first, ((w1_ref, "all"), (w1m_ref, "middle")))
-    build_weights(inner, second, ((w2a_ref, "low"), (w2b_ref, "high")))
+    build_weights(inner, conv_ref, 0, ((w1_ref, "all"), (w1m_ref, "middle")))
+    build_weights(inner, conv_ref, 1, ((w2a_ref, "low"), (w2b_ref, "high")))
     lift(slab_ref, x1_ref, par_ref)
     bias = bias_of(par_ref, 2)
     for at in range(0, NX, CHUNK):
@@ -197,7 +195,8 @@
                 for pair in range(1, 8):
                     total = total + terms[pair * 8 : pair * 8 + 8]
                 z = 2 + len(slices)
-                base = left_ref[z, :, at : at + CHUNK] if z < DEPTH else own_ref[z - DEPTH, :, at : at + CHUNK]
+                cells_ref = left_ref if z < DEPTH else own_ref
+                base = cells_ref[z % DEPTH, :, at : at + CHUNK].astype(F32)
                 slices.append(base + total[0:4] + total[4:8])
         mixed = jnp.concatenate([slices[z][y : y + 1] for y in range(NY) for z in range(DEPTH)], 0)
         a += [mixed[:, i : i + INNER] for i in range(0, CHUNK, INNER)]
@@ -363,16 +362,16 @@
     ahead, back = z_tables()
     place = lax.axis_index("gz")
     slab = density[0]
-    left = lax.ppermute(slab, "gz", [(i, (i + 1) % GZ) for i in range(GZ)])
-
-    flat = lambda w: w.transpose(2, 3, 4, 0, 1).reshape(27 * CH, CH)
+    rounded = slab.astype(BF16)
+    left = lax.ppermute(rounded, "gz", [(i, (i + 1) % GZ) for i in range(GZ)])
+
     at = place.astype(jnp.int32).reshape(1)
     vectors = jnp.stack([lift_weight, lift_bias, bias_first, bias_second, projection])
-    small = jnp.concatenate([flat(conv_first).astype(F32), flat(conv_second).astype(F32), vectors], 0)
+    convs = jnp.concatenate([conv_first, conv_second], 0).transpose(2, 3, 4, 0, 1).reshape(54 * CH, CH)
     par, w1, w1m, w2a, w2b, x1, x2 = call(
         prepare_kernel,
         [shape(5, 4 * CH, INNER, dtype=F32)] + [shape(128, 768)] * 4 + [shape(3, 256, NX), shape(3, 128, NX)],
-        at, slab, small, smem=1, megabytes=24, flops=10**9,
+        at, rounded, convs, vectors, smem=1, megabytes=24, flops=10**9,
     )
     plus, minus = call(
         wedge_kernel, [shape(NZ, INNER, dtype=F32)] * 2, at, wedge, smem=1, megabytes=16, flops=10**9,

time: 59.3 us -> 56.6 us (0.954)
  blocking collectives: 35.4 us -> 34.2 us
  local copies, waits for them, and re-layouts: 1.76 us -> 0.79 us
    all_to_all x1, blocking collectives: 20.5 us -> 19.3 us  [body(): lax.all_to_all(spectrum, 'gz', split_axis=0, concat_axis=0, tiled=True)]
    concatenate x0 -> x1, other arithmetic: none -> 1 us  [body(): jnp.concatenate([conv_first, conv_second], 0).transpose(2, 3, 4, 0, 1)]
    convert_element_type x2 -> x1, other arithmetic: 1.83 us -> 0.93 us  [body(): rounded = slab.astype(BF16)]
    unnamed x18, local copies, waits for them, and re-layouts: 0.95 us -> 0.05 us
    concatenate x1 -> x0, local copies, waits for them, and re-layouts: 0.81 us -> none  [body(): jnp.concatenate([flat(conv_first).astype(F32), flat(conv_second).astype(F...]
    another operation x0 -> x1, local copies, waits for them, and re-layouts: none -> 0.74 us  [body(): jnp.stack([lift_weight, lift_bias, bias_first, bias_second, projection])]
  transfers between devices with their start and end apart: 2 -> 2, of which waited for: 1 -> 1; matrix products, arithmetic and copies ran while one was open for 4% -> 3% of each run, Pallas kernels for 6% -> 6%
where the time goes in v3:
time: 56.6 us; the launch traced here: 56.4 us
  blocking collectives  34.2 us (60%)
  Pallas kernels  7.87 us (14%)
  starting transfers between devices  6.25 us (11%)
  waiting for transfers between devices  5.25 us (9%)
  other arithmetic  1.92 us (3%)
  local copies, waits for them, and re-layouts  0.79 us (1%)
    all_to_all x1, blocking collectives, body(): lax.all_to_all(spectrum, 'gz', split_axis=0, concat_axis=0, tiled=True)  19.3 us
    all_to_all x1, blocking collectives, body(): lax.all_to_all(returned.reshape(GZ, DEPTH, INNER), 'gz', split_axis=0, co...  14.9 us
    pallas_call x5, Pallas kernels, call(): pl.pallas_call(kernel, out_shape=outs, in_specs=[spec(pltpu.SMEM)] * smem...  7.87 us
    ppermute x1, waiting for transfers between devices, body(): left = lax.ppermute(rounded, 'gz', [(i, (i + 1) % GZ) for i in range(GZ)])  5.24 us
    ppermute x1, starting transfers between devices, body(): left = lax.ppermute(rounded, 'gz', [(i, (i + 1) % GZ) for i in range(GZ)])  3.9 us
    ppermute x1, starting transfers between devices, body(): lax.ppermute(pencils, 'half', [(i, i ^ 1) for i in range(lax.axis_size('h...  2.36 us
  transfers between devices with their start and end apart: 2, of which 1 were waited for; matrix products, arithmetic and copies ran while one was open for 3% of the time, Pallas kernels for 6%

profile of v3, /device:TPU:1, one launch (start us, length us, event | category | flops | bytes accessed | tf_op | source)
XLA Modules:
  0.0 56.4 jit_solution(2664439446538153045)
XLA Ops:
  0.0 0.9 %bitcast_convert_fusion.slab_ref = bf16[4,4,2048]{2,1,0:T(4,128)(2,1)S(1)} fusion(f32[1,4,4,2048]{3,2,1,0:T(4,128)} %param.16), kind=kLoop, calls=%fused_computation.1 | loop fusion | flops 32768 | bytes 196608 | tf_op jit(solution)/shard_map/convert_element_type | solution.py:365
  0.9 0.0 copy-start
  0.9 0.0 copy-start.4
  1.0 0.0 copy-start.5
  1.0 0.0 copy-start.7
  1.0 3.9 %collective-permute-start = (bf16[4,4,2048]{2,1,0:T(4,128)(2,1)S(1)}, bf16[4,4,2048]{2,1,0:T(4,128)(2,1)S(1)}, u32[]{:S(2)}, u32[]{:S(2)}) collective-permute-start(bf16[4,4,2048]{2,1,0:T(4,128)(2,1)S(1)} %bitcast_convert_fusion.slab_ref), channel_id=1, source_target_pairs={{0,1},{1,2},{2,3},{3,4},{4,5},{5,6},{6,7},{7,8},{8,9},{9,10},{10,1... | collective-permute-start | bytes 196616 | tf_op jit(solution)/shard_map/ppermute | solution.py:366
  4.9 1.0 %pad_maximum_fusion = bf16[32,16,3,3,3]{1,0,4,3,2:T(8,128)(2,1)S(1)} fusion(bf16[16,16,3,3,3]{1,0,4,3,2:T(8,128)(2,1)} %param.21, bf16[16,16,3,3,3]{1,0,4,3,2:T(8,128)(2,1)} %param.19), kind=kLoop, calls=%fused_computation | loop fusion | flops 55296 | bytes 55296 | tf_op jit(solution)/shard_map/concatenate | solution.py:370
  5.9 0.7 %stack.23.vector_ref = f32[5,16]{1,0:T(8,128)S(1)} concatenate(f32[1,16]{1,0:T(1,128)} %bitcast.19, f32[1,16]{1,0:T(1,128)} %bitcast.20, f32[1,16]{1,0:T(1,128)} %bitcast.21, f32[1,16]{1,0:T(1,128)} %bitcast.22, f32[1,16]{1,0:T(1,128)} %bitcast.23), dimensions={0} | concatenate | bytes 640 | tf_op jit(solution)/shard_map/stack | solution.py:369
  6.6 2.4 %shard_map.154 = (f32[5,64,128]{2,1,0:T(8,128)S(1)}, bf16[128,768]{1,0:T(8,128)(2,1)S(1)}, bf16[128,768]{1,0:T(8,128)(2,1)S(1)}, bf16[128,768]{1,0:T(8,128)(2,1)...) custom-call(s32[1]{0:T(128)} %bitcast.1.at_ref, ...), custom_call_target="tpu_custom_call" | custom-call | flops 1000000000 | bytes 93508 | tf_op jit(solution)/shard_map/pallas_call | solution.py:335
  9.1 5.2 %collective-permute-done.left_ref = bf16[4,4,2048]{2,1,0:T(4,128)(2,1)S(1)} collective-permute-done((bf16[4,4,2048]{2,1,0:T(4,128)(2,1)S(1)}, bf16[4,4,2048]{2,1,0:T(4,128)(2,1)S(1)}, u32[]{:S(2)}, u32[]{:S(2)}) %collective-permute-start) | collective-permute-done | bytes 65568 | tf_op jit(solution)/shard_map/ppermute | solution.py:366
  14.3 0.0 copy-done
  14.3 0.0 copy-done.4
  14.3 0.0 copy-done.5
  14.3 0.0 copy-done.7
  14.3 0.0 copy-start.8
  14.3 2.7 %shard_map.155 = bf16[64,4,128]{2,1,0:T(4,128)(2,1)S(1)} custom-call(bf16[4,4,2048]{2,1,0:T(4,128)(2,1)S(1)} %collective-permute-done.left_ref, f32[4,4,2048]{2,1,0:T(4,128)S(1)} %bitcast.14, f32[5,64,128]{2,1,0:T(8,128)S(1)} %get-tuple-element.14.par_ref, bf16[128,768]{1,0:T(8,128)(2,1)S(1)} %get-tuple-element.15.w1_ref, ...), custom_call_target="tpu_custom_call" | custom-call | flops 1000000000 | bytes 6070272 | tf_op jit(solution)/shard_map/pallas_call | solution.py:335
  17.0 0.0 copy-start.1
  17.0 0.0 copy-start.2
  17.0 19.3 %all_to_all.10 = bf16[64,4,128]{2,1,0:T(4,128)(2,1)S(1)} all-to-all(bf16[64,4,128]{2,1,0:T(4,128)(2,1)S(1)} %shard_map.155), channel_id=1, replica_groups=mesh['half'=4,'gz'=64] {'gz'}, dimensions={0} | all-to-all | bytes 131072 | tf_op jit(solution)/shard_map/all_to_all | solution.py:385
  36.3 0.0 copy-start.3
  36.3 0.0 copy-start.6
  36.3 2.4 %collective-permute-start.1 = (bf16[256,128]{1,0:T(8,128)(2,1)S(1)}, bf16[256,128]{1,0:T(8,128)(2,1)S(1)}, u32[]{:S(2)}, u32[]{:S(2)}) collective-permute-start(bf16[256,128]{1,0:T(8,128)(2,1)S(1)} %bitcast.15), channel_id=1, source_target_pairs={{0,64},{64,0},{128,192},{192,128},{1,65},{65,1},{129,193},{193,129... | collective-permute-start | bytes 196616 | tf_op jit(solution)/shard_map/ppermute | solution.py:387
  38.7 0.0 copy-done.8
  38.7 1.2 %shard_map.156 = (f32[256,128]{1,0:T(8,128)S(1)}, f32[256,128]{1,0:T(8,128)S(1)}) custom-call(s32[1]{0:T(128)} %bitcast.1.at_ref, f32[256,2048]{1,0:T(8,128)S(1)} %copy-done.8), custom_call_target="tpu_custom_call" | custom-call | flops 1000000000 | bytes 2097156 | tf_op jit(solution)/shard_map/pallas_call | solution.py:335
  39.9 0.0 collective-permute-done.1.other_ref
  39.9 0.0 copy-done.1
  39.9 0.0 copy-done.2
  39.9 0.7 %shard_map.157 = bf16[256,128]{1,0:T(8,128)(2,1)S(1)} custom-call(bf16[256,128]{1,0:T(8,128)(2,1)S(1)} %bitcast.16, bf16[256,128]{1,0:T(8,128)(2,1)S(1)} %collective-permute-done.1.other_ref, f32[256,128]{1,0:T(8,128)S(1)} %get-tuple-element.21.plus_ref, f32[256,128]{1,0:T(8,128)S(1)} %get-tuple-element.22.minus_ref, bf16[512,256]{1,0:T(8,128)(2,1)S(1)} %copy-done.1, ...), custom_call_target="tpu_custom_call" | custom-call | flops 10000000 | bytes 917504 | tf_op jit(solution)/shard_map/pallas_call | solution.py:335
  40.6 14.9 %all_to_all.11.in_ref = bf16[64,4,128]{2,1,0:T(4,128)(2,1)S(1)} all-to-all(bf16[64,4,128]{2,1,0:T(4,128)(2,1)S(1)} %bitcast.17), channel_id=1, replica_groups=mesh['half'=4,'gz'=64] {'gz'}, dimensions={0} | all-to-all | bytes 131072 | tf_op jit(solution)/shard_map/all_to_all | solution.py:391
  55.4 0.0 copy-done.3
  55.5 0.0 copy-done.6
  55.5 0.9 %shard_map.158 = f32[4,4,2048]{2,1,0:T(4,128)} custom-call(bf16[64,4,128]{2,1,0:T(4,128)(2,1)S(1)} %all_to_all.11.in_ref, bf16[256,256]{1,0:T(8,128)(2,1)S(1)} %copy-done.3, bf16[128,256]{1,0:T(8,128)(2,1)S(1)} %copy-done.6, f32[16,128]{1,0:T(8,128)S(1)} %copy-done.7), custom_call_target="tpu_custom_call" | custom-call | flops 10000000 | bytes 270336 | tf_op jit(solution)/shard_map/pallas_call | solution.py:335
Async XLA Ops:
  0.9 13.4 %copy-start = (f32[1,4,4,2048]{3,2,1,0:T(4,128)S(1)}, f32[1,4,4,2048]{3,2,1,0:T(4,128)}, u32[]{:S(2)}) copy-start(f32[1,4,4,2048]{3,2,1,0:T(4,128)} %param.16) | copy-start | bytes 393220
  0.9 13.4 %copy-start.4 = (bf16[256,256]{1,0:T(8,128)(2,1)S(1)}, bf16[256,256]{1,0:T(8,128)(2,1)}, u32[]{:S(2)}) copy-start(bf16[256,256]{1,0:T(8,128)(2,1)} %constant.18.clone.full_ref) | copy-start | bytes 393220
  1.0 13.4 %copy-start.5 = (bf16[128,256]{1,0:T(8,128)(2,1)S(1)}, bf16[128,256]{1,0:T(8,128)(2,1)}, u32[]{:S(2)}) copy-start(bf16[128,256]{1,0:T(8,128)(2,1)} %constant.19.clone.ends_ref) | copy-start | bytes 196612
  1.0 13.4 %copy-start.7 = (f32[16,128]{1,0:T(8,128)S(1)}, f32[16,128]{1,0:T(8,128)}, u32[]{:S(2)}) copy-start(f32[16,128]{1,0:T(8,128)} %constant.20.clone.twiddle_ref) | copy-start | bytes 24580
  1.0 13.3 %collective-permute-start = (bf16[4,4,2048]{2,1,0:T(4,128)(2,1)S(1)}, bf16[4,4,2048]{2,1,0:T(4,128)(2,1)S(1)}, u32[]{:S(2)}, u32[]{:S(2)}) collective-permute-start(bf16[4,4,2048]{2,1,0:T(4,128)(2,1)S(1)} %bitcast_convert_fusion.slab_ref), channel_id=1, source_target_pairs={{0,1},{1,2},{2,3},{3,4},{4,5},{5,6},{6,7},{7,8},{8,9},{9,10},{10,1... | collective-permute-start | bytes 196616 | tf_op jit(solution)/shard_map/ppermute | solution.py:366
  14.3 24.4 %copy-start.8 = (f32[256,2048]{1,0:T(8,128)S(1)}, f32[256,2048]{1,0:T(8,128)}, u32[]{:S(2)}) copy-start(f32[256,2048]{1,0:T(8,128)} %wedge_ref.1) | copy-start | bytes 6291460
  17.0 22.9 %copy-start.1 = (bf16[512,256]{1,0:T(8,128)(2,1)S(1)}, bf16[512,256]{1,0:T(8,128)(2,1)}, u32[]{:S(2)}) copy-start(bf16[512,256]{1,0:T(8,128)(2,1)} %constant.21.clone.ahead_ref) | copy-start | bytes 786436
  17.0 22.9 %copy-start.2 = (bf16[512,256]{1,0:T(8,128)(2,1)S(1)}, bf16[512,256]{1,0:T(8,128)(2,1)}, u32[]{:S(2)}) copy-start(bf16[512,256]{1,0:T(8,128)(2,1)} %constant.22.clone.back_ref) | copy-start | bytes 786436
  36.3 19.1 %copy-start.3 = (bf16[256,256]{1,0:T(8,128)(2,1)S(1)}, bf16[256,256]{1,0:T(8,128)(2,1)}, u32[]{:S(2)}) copy-start(bf16[256,256]{1,0:T(8,128)(2,1)} %constant.23.clone.full_ref) | copy-start | bytes 393220
  36.3 19.1 %copy-start.6 = (bf16[128,256]{1,0:T(8,128)(2,1)S(1)}, bf16[128,256]{1,0:T(8,128)(2,1)}, u32[]{:S(2)}) copy-start(bf16[128,256]{1,0:T(8,128)(2,1)} %constant.24.clone.ends_ref) | copy-start | bytes 196612
  36.3 3.5 %collective-permute-start.1 = (bf16[256,128]{1,0:T(8,128)(2,1)S(1)}, bf16[256,128]{1,0:T(8,128)(2,1)S(1)}, u32[]{:S(2)}, u32[]{:S(2)}) collective-permute-start(bf16[256,128]{1,0:T(8,128)(2,1)S(1)} %bitcast.15), channel_id=1, source_target_pairs={{0,64},{64,0},{128,192},{192,128},{1,65},{65,1},{129,193},{193,129... | collective-permute-start | bytes 196616 | tf_op jit(solution)/shard_map/ppermute | solution.py:387

commit v4 on v3

--- a/solution.py
+++ b/solution.py
@@ -16,6 +16,13 @@
 BLOCKS = 16
 LAG = 2
 F32, BF16 = jnp.float32, jnp.bfloat16
+ORDER = (
+    46, 24, 10, 23, 29, 15, 43, 25, 3, 9, 1, 17, 8, 58, 26, 4,
+    50, 42, 41, 38, 62, 14, 33, 5, 21, 31, 28, 57, 44, 18, 51, 34,
+    45, 61, 54, 22, 35, 11, 20, 39, 32, 12, 47, 7, 37, 6, 27, 36,
+    56, 52, 16, 63, 2, 30, 40, 19, 55, 13, 0, 60, 53, 59, 49, 48,
+)
+RANK = tuple(ORDER.index(i) for i in range(GZ))
 
 
 def dot(a, b):
@@ -56,10 +63,10 @@
 
 
 def z_tables():
-    kz = np.arange(NZ)[:, None]
-    row = np.arange(NZ)[None, :]
-    ahead = np.concatenate(turn(kz * (row - LAG), NZ), 0)
-    back = np.concatenate(turn(kz * row, NZ), 0)
+    kz = np.arange(NZ)
+    z = (DEPTH * np.array(ORDER)[:, None] + np.arange(DEPTH)[None, :]).reshape(NZ)
+    ahead = np.concatenate(turn(kz[:, None] * (z - LAG)[None, :], NZ), 0)
+    back = np.concatenate(turn(z[:, None] * kz[None, :], NZ), 0)
     return ahead.astype(jnp.bfloat16), back.astype(jnp.bfloat16)
 
 
@@ -247,12 +254,12 @@
             blocks.append(whole[(k1 - 1) * 16 : k1 * 16, h * INNER : (h + 1) * INNER])
     for y in range(NY):
         for b in range(BLOCKS):
-            out_ref[y * BLOCKS + b] = blocks[b][y * DEPTH : (y + 1) * DEPTH].astype(BF16)
+            out_ref[RANK[y * BLOCKS + b]] = blocks[b][y * DEPTH : (y + 1) * DEPTH].astype(BF16)
 
 
 def inverse_kernel(in_ref, full_ref, ends_ref, twiddle_ref, out_ref):
     blocks = [
-        jnp.concatenate([in_ref[y * BLOCKS + b].astype(F32) for y in range(NY)], 0).astype(BF16)
+        jnp.concatenate([in_ref[RANK[y * BLOCKS + b]].astype(F32) for y in range(NY)], 0).astype(BF16)
         for b in range(BLOCKS)
     ]
     even = dot(blocks[0], ends_ref[:, :INNER])
@@ -343,6 +350,12 @@
     )(*args)
 
 
+def exchange(chunks):
+    return lax.all_to_all(
+        chunks, "gz", split_axis=0, concat_axis=0, tiled=True, axis_index_groups=[list(ORDER)]
+    )
+
+
 def shape(*dims, dtype=BF16):
     return jax.ShapeDtypeStruct(dims, dtype)
 
@@ -382,15 +395,12 @@
         scratch=[pltpu.VMEM((3, 256, NX), BF16), pltpu.VMEM((3, 256, NX), BF16)],
         megabytes=24, flops=10**9,
     )
-    pencils = lax.all_to_all(spectrum, "gz", split_axis=0, concat_axis=0, tiled=True)
-    pencils = pencils.reshape(NZ, INNER)
+    pencils = exchange(spectrum).reshape(NZ, INNER)
     other = lax.ppermute(pencils, "half", [(i, i ^ 1) for i in range(lax.axis_size("half"))])
     returned = call(
         middle_kernel, shape(NZ, INNER), pencils, other, plus, minus, ahead, back,
     )
-    slabs = lax.all_to_all(
-        returned.reshape(GZ, DEPTH, INNER), "gz", split_axis=0, concat_axis=0, tiled=True
-    )
+    slabs = exchange(returned.reshape(GZ, DEPTH, INNER))
     residual = call(
         inverse_kernel, shape(DEPTH, NY, NX, dtype=F32), slabs, full_i, ends_i, twiddle,
     )

time: 56.6 us -> 52.3 us (0.924)
  blocking collectives: 34.2 us -> 29.4 us
    all_to_all x2, blocking collectives: 34.2 us -> 29.4 us  [exchange(): lax.all_to_all(chunks, 'gz', split_axis=0, concat_axis=0, tiled=True, axi...]
  transfers between devices with their start and end apart: 2 -> 2, of which waited for: 1 -> 1; matrix products, arithmetic and copies ran while one was open for 3% -> 3% of each run, Pallas kernels for 6% -> 7%
where the time goes in v4:
time: 52.3 us; the launch traced here: 52 us
  blocking collectives  29.4 us (56%)
  Pallas kernels  7.88 us (15%)
  starting transfers between devices  6.63 us (13%)
  waiting for transfers between devices  5.25 us (10%)
  other arithmetic  1.92 us (4%)
  local copies, waits for them, and re-layouts  0.79 us (2%)
    all_to_all x2, blocking collectives, exchange(): lax.all_to_all(chunks, 'gz', split_axis=0, concat_axis=0, tiled=True, axi...  29.4 us
    pallas_call x5, Pallas kernels, call(): pl.pallas_call(kernel, out_shape=outs, in_specs=[spec(pltpu.SMEM)] * smem...  7.88 us
    ppermute x1, waiting for transfers between devices, body(): left = lax.ppermute(rounded, 'gz', [(i, (i + 1) % GZ) for i in range(GZ)])  5.24 us
    ppermute x1, starting transfers between devices, body(): left = lax.ppermute(rounded, 'gz', [(i, (i + 1) % GZ) for i in range(GZ)])  3.9 us
    ppermute x1, starting transfers between devices, body(): lax.ppermute(pencils, 'half', [(i, i ^ 1) for i in range(lax.axis_size('h...  2.73 us
  transfers between devices with their start and end apart: 2, of which 1 were waited for; matrix products, arithmetic and copies ran while one was open for 3% of the time, Pallas kernels for 7%

profile of v4, /device:TPU:1, one launch (start us, length us, event | category | flops | bytes accessed | tf_op | source)
XLA Modules:
  0.0 52.0 jit_solution(11343613107596302838)
XLA Ops:
  0.0 0.9 %bitcast_convert_fusion.slab_ref = bf16[4,4,2048]{2,1,0:T(4,128)(2,1)S(1)} fusion(f32[1,4,4,2048]{3,2,1,0:T(4,128)} %param.16), kind=kLoop, calls=%fused_computation.1 | loop fusion | flops 32768 | bytes 196608 | tf_op jit(solution)/shard_map/convert_element_type | solution.py:378
  0.9 0.0 copy-start
  0.9 0.0 copy-start.4
  1.0 0.0 copy-start.5
  1.0 0.0 copy-start.7
  1.0 3.9 %collective-permute-start = (bf16[4,4,2048]{2,1,0:T(4,128)(2,1)S(1)}, bf16[4,4,2048]{2,1,0:T(4,128)(2,1)S(1)}, u32[]{:S(2)}, u32[]{:S(2)}) collective-permute-start(bf16[4,4,2048]{2,1,0:T(4,128)(2,1)S(1)} %bitcast_convert_fusion.slab_ref), channel_id=1, source_target_pairs={{0,1},{1,2},{2,3},{3,4},{4,5},{5,6},{6,7},{7,8},{8,9},{9,10},{10,1... | collective-permute-start | bytes 196616 | tf_op jit(solution)/shard_map/ppermute | solution.py:379
  4.9 1.0 %pad_maximum_fusion = bf16[32,16,3,3,3]{1,0,4,3,2:T(8,128)(2,1)S(1)} fusion(bf16[16,16,3,3,3]{1,0,4,3,2:T(8,128)(2,1)} %param.21, bf16[16,16,3,3,3]{1,0,4,3,2:T(8,128)(2,1)} %param.19), kind=kLoop, calls=%fused_computation | loop fusion | flops 55296 | bytes 55296 | tf_op jit(solution)/shard_map/concatenate | solution.py:383
  5.9 0.7 %stack.23.vector_ref = f32[5,16]{1,0:T(8,128)S(1)} concatenate(f32[1,16]{1,0:T(1,128)} %bitcast.19, f32[1,16]{1,0:T(1,128)} %bitcast.20, f32[1,16]{1,0:T(1,128)} %bitcast.21, f32[1,16]{1,0:T(1,128)} %bitcast.22, f32[1,16]{1,0:T(1,128)} %bitcast.23), dimensions={0} | concatenate | bytes 640 | tf_op jit(solution)/shard_map/stack | solution.py:382
  6.6 2.4 %shard_map.154 = (f32[5,64,128]{2,1,0:T(8,128)S(1)}, bf16[128,768]{1,0:T(8,128)(2,1)S(1)}, bf16[128,768]{1,0:T(8,128)(2,1)S(1)}, bf16[128,768]{1,0:T(8,128)(2,1)...) custom-call(s32[1]{0:T(128)} %bitcast.1.at_ref, ...), custom_call_target="tpu_custom_call" | custom-call | flops 1000000000 | bytes 93508 | tf_op jit(solution)/shard_map/pallas_call | solution.py:342
  9.1 5.2 %collective-permute-done.left_ref = bf16[4,4,2048]{2,1,0:T(4,128)(2,1)S(1)} collective-permute-done((bf16[4,4,2048]{2,1,0:T(4,128)(2,1)S(1)}, bf16[4,4,2048]{2,1,0:T(4,128)(2,1)S(1)}, u32[]{:S(2)}, u32[]{:S(2)}) %collective-permute-start) | collective-permute-done | bytes 65568 | tf_op jit(solution)/shard_map/ppermute | solution.py:379
  14.3 0.0 copy-done
  14.3 0.0 copy-done.4
  14.3 0.0 copy-done.5
  14.3 0.0 copy-done.7
  14.3 0.0 copy-start.8
  14.3 2.7 %shard_map.155 = bf16[64,4,128]{2,1,0:T(4,128)(2,1)S(1)} custom-call(bf16[4,4,2048]{2,1,0:T(4,128)(2,1)S(1)} %collective-permute-done.left_ref, f32[4,4,2048]{2,1,0:T(4,128)S(1)} %bitcast.14, f32[5,64,128]{2,1,0:T(8,128)S(1)} %get-tuple-element.14.par_ref, bf16[128,768]{1,0:T(8,128)(2,1)S(1)} %get-tuple-element.15.w1_ref, ...), custom_call_target="tpu_custom_call" | custom-call | flops 1000000000 | bytes 6070272 | tf_op jit(solution)/shard_map/pallas_call | solution.py:342
  17.0 0.0 copy-start.1
  17.0 0.0 copy-start.2
  17.0 14.5 %all_to_all.10 = bf16[64,4,128]{2,1,0:T(4,128)(2,1)S(1)} all-to-all(bf16[64,4,128]{2,1,0:T(4,128)(2,1)S(1)} %shard_map.155), channel_id=1, replica_groups={{46,24,10,23,29,15,43,25,3,9,1,17,8,58,26,4,50,42,41,38,62,14,33,5,21,3..., dimensions={0} | all-to-all | bytes 131072 | tf_op jit(solution)/shard_map/all_to_all | solution.py:354
  31.6 0.0 copy-start.3
  31.6 0.0 copy-start.6
  31.6 2.7 %collective-permute-start.1 = (bf16[256,128]{1,0:T(8,128)(2,1)S(1)}, bf16[256,128]{1,0:T(8,128)(2,1)S(1)}, u32[]{:S(2)}, u32[]{:S(2)}) collective-permute-start(bf16[256,128]{1,0:T(8,128)(2,1)S(1)} %bitcast.15), channel_id=1, source_target_pairs={{0,64},{64,0},{128,192},{192,128},{1,65},{65,1},{129,193},{193,129... | collective-permute-start | bytes 196616 | tf_op jit(solution)/shard_map/ppermute | solution.py:399
  34.3 0.0 copy-done.8
  34.3 1.2 %shard_map.156 = (f32[256,128]{1,0:T(8,128)S(1)}, f32[256,128]{1,0:T(8,128)S(1)}) custom-call(s32[1]{0:T(128)} %bitcast.1.at_ref, f32[256,2048]{1,0:T(8,128)S(1)} %copy-done.8), custom_call_target="tpu_custom_call" | custom-call | flops 1000000000 | bytes 2097156 | tf_op jit(solution)/shard_map/pallas_call | solution.py:342
  35.5 0.0 collective-permute-done.1.other_ref
  35.5 0.0 copy-done.1
  35.5 0.0 copy-done.2
  35.5 0.7 %shard_map.157 = bf16[256,128]{1,0:T(8,128)(2,1)S(1)} custom-call(bf16[256,128]{1,0:T(8,128)(2,1)S(1)} %bitcast.16, bf16[256,128]{1,0:T(8,128)(2,1)S(1)} %collective-permute-done.1.other_ref, f32[256,128]{1,0:T(8,128)S(1)} %get-tuple-element.21.plus_ref, f32[256,128]{1,0:T(8,128)S(1)} %get-tuple-element.22.minus_ref, bf16[512,256]{1,0:T(8,128)(2,1)S(1)} %copy-done.1, ...), custom_call_target="tpu_custom_call" | custom-call | flops 10000000 | bytes 917504 | tf_op jit(solution)/shard_map/pallas_call | solution.py:342
  36.2 14.9 %all_to_all.11.in_ref = bf16[64,4,128]{2,1,0:T(4,128)(2,1)S(1)} all-to-all(bf16[64,4,128]{2,1,0:T(4,128)(2,1)S(1)} %bitcast.17), channel_id=1, replica_groups={{46,24,10,23,29,15,43,25,3,9,1,17,8,58,26,4,50,42,41,38,62,14,33,5,21,3..., dimensions={0} | all-to-all | bytes 131072 | tf_op jit(solution)/shard_map/all_to_all | solution.py:354
  51.1 0.0 copy-done.3
  51.1 0.0 copy-done.6
  51.1 0.9 %shard_map.158 = f32[4,4,2048]{2,1,0:T(4,128)} custom-call(bf16[64,4,128]{2,1,0:T(4,128)(2,1)S(1)} %all_to_all.11.in_ref, bf16[256,256]{1,0:T(8,128)(2,1)S(1)} %copy-done.3, bf16[128,256]{1,0:T(8,128)(2,1)S(1)} %copy-done.6, f32[16,128]{1,0:T(8,128)S(1)} %copy-done.7), custom_call_target="tpu_custom_call" | custom-call | flops 10000000 | bytes 270336 | tf_op jit(solution)/shard_map/pallas_call | solution.py:342
Async XLA Ops:
  0.9 13.4 %copy-start = (f32[1,4,4,2048]{3,2,1,0:T(4,128)S(1)}, f32[1,4,4,2048]{3,2,1,0:T(4,128)}, u32[]{:S(2)}) copy-start(f32[1,4,4,2048]{3,2,1,0:T(4,128)} %param.16) | copy-start | bytes 393220
  0.9 13.4 %copy-start.4 = (bf16[256,256]{1,0:T(8,128)(2,1)S(1)}, bf16[256,256]{1,0:T(8,128)(2,1)}, u32[]{:S(2)}) copy-start(bf16[256,256]{1,0:T(8,128)(2,1)} %constant.18.clone.full_ref) | copy-start | bytes 393220
  1.0 13.4 %copy-start.5 = (bf16[128,256]{1,0:T(8,128)(2,1)S(1)}, bf16[128,256]{1,0:T(8,128)(2,1)}, u32[]{:S(2)}) copy-start(bf16[128,256]{1,0:T(8,128)(2,1)} %constant.19.clone.ends_ref) | copy-start | bytes 196612
  1.0 13.4 %copy-start.7 = (f32[16,128]{1,0:T(8,128)S(1)}, f32[16,128]{1,0:T(8,128)}, u32[]{:S(2)}) copy-start(f32[16,128]{1,0:T(8,128)} %constant.20.clone.twiddle_ref) | copy-start | bytes 24580
  1.0 13.3 %collective-permute-start = (bf16[4,4,2048]{2,1,0:T(4,128)(2,1)S(1)}, bf16[4,4,2048]{2,1,0:T(4,128)(2,1)S(1)}, u32[]{:S(2)}, u32[]{:S(2)}) collective-permute-start(bf16[4,4,2048]{2,1,0:T(4,128)(2,1)S(1)} %bitcast_convert_fusion.slab_ref), channel_id=1, source_target_pairs={{0,1},{1,2},{2,3},{3,4},{4,5},{5,6},{6,7},{7,8},{8,9},{9,10},{10,1... | collective-permute-start | bytes 196616 | tf_op jit(solution)/shard_map/ppermute | solution.py:379
  14.3 20.0 %copy-start.8 = (f32[256,2048]{1,0:T(8,128)S(1)}, f32[256,2048]{1,0:T(8,128)}, u32[]{:S(2)}) copy-start(f32[256,2048]{1,0:T(8,128)} %wedge_ref.1) | copy-start | bytes 6291460
  17.0 18.5 %copy-start.1 = (bf16[512,256]{1,0:T(8,128)(2,1)S(1)}, bf16[512,256]{1,0:T(8,128)(2,1)}, u32[]{:S(2)}) copy-start(bf16[512,256]{1,0:T(8,128)(2,1)} %constant.21.clone.ahead_ref) | copy-start | bytes 786436
  17.0 18.5 %copy-start.2 = (bf16[512,256]{1,0:T(8,128)(2,1)S(1)}, bf16[512,256]{1,0:T(8,128)(2,1)}, u32[]{:S(2)}) copy-start(bf16[512,256]{1,0:T(8,128)(2,1)} %constant.22.clone.back_ref) | copy-start | bytes 786436
  31.6 19.5 %copy-start.3 = (bf16[256,256]{1,0:T(8,128)(2,1)S(1)}, bf16[256,256]{1,0:T(8,128)(2,1)}, u32[]{:S(2)}) copy-start(bf16[256,256]{1,0:T(8,128)(2,1)} %constant.23.clone.full_ref) | copy-start | bytes 393220
  31.6 19.5 %copy-start.6 = (bf16[128,256]{1,0:T(8,128)(2,1)S(1)}, bf16[128,256]{1,0:T(8,128)(2,1)}, u32[]{:S(2)}) copy-start(bf16[128,256]{1,0:T(8,128)(2,1)} %constant.24.clone.ends_ref) | copy-start | bytes 196612
  31.6 3.9 %collective-permute-start.1 = (bf16[256,128]{1,0:T(8,128)(2,1)S(1)}, bf16[256,128]{1,0:T(8,128)(2,1)S(1)}, u32[]{:S(2)}, u32[]{:S(2)}) collective-permute-start(bf16[256,128]{1,0:T(8,128)(2,1)S(1)} %bitcast.15), channel_id=1, source_target_pairs={{0,64},{64,0},{128,192},{192,128},{1,65},{65,1},{129,193},{193,129... | collective-permute-start | bytes 196616 | tf_op jit(solution)/shard_map/ppermute | solution.py:399

commit v5 on v4

--- a/solution.py
+++ b/solution.py
@@ -16,13 +16,20 @@
 BLOCKS = 16
 LAG = 2
 F32, BF16 = jnp.float32, jnp.bfloat16
-ORDER = (
-    46, 24, 10, 23, 29, 15, 43, 25, 3, 9, 1, 17, 8, 58, 26, 4,
-    50, 42, 41, 38, 62, 14, 33, 5, 21, 31, 28, 57, 44, 18, 51, 34,
-    45, 61, 54, 22, 35, 11, 20, 39, 32, 12, 47, 7, 37, 6, 27, 36,
-    56, 52, 16, 63, 2, 30, 40, 19, 55, 13, 0, 60, 53, 59, 49, 48,
+FORTH = (
+    34, 47, 16, 38, 36, 54, 4, 52, 51, 48, 45, 20, 7, 50, 30, 49,
+    44, 15, 58, 35, 10, 9, 55, 25, 18, 11, 40, 42, 62, 41, 21, 23,
+    2, 13, 3, 61, 56, 32, 43, 26, 31, 60, 6, 59, 29, 39, 14, 0,
+    28, 17, 12, 46, 8, 22, 33, 24, 27, 19, 63, 1, 5, 53, 57, 37,
 )
-RANK = tuple(ORDER.index(i) for i in range(GZ))
+BACK = (
+    42, 58, 26, 38, 46, 22, 62, 41, 10, 30, 34, 43, 54, 47, 50, 6,
+    57, 25, 14, 27, 45, 37, 39, 59, 18, 53, 33, 29, 23, 11, 63, 2,
+    35, 21, 40, 9, 31, 55, 61, 44, 49, 15, 56, 7, 24, 36, 13, 17,
+    19, 5, 51, 32, 1, 3, 60, 52, 8, 28, 20, 4, 16, 48, 12, 0,
+)
+FORTH_RANK = tuple(FORTH.index(i) for i in range(GZ))
+BACK_RANK = tuple(BACK.index(i) for i in range(GZ))
 
 
 def dot(a, b):
@@ -64,9 +71,9 @@
 
 def z_tables():
     kz = np.arange(NZ)
-    z = (DEPTH * np.array(ORDER)[:, None] + np.arange(DEPTH)[None, :]).reshape(NZ)
-    ahead = np.concatenate(turn(kz[:, None] * (z - LAG)[None, :], NZ), 0)
-    back = np.concatenate(turn(z[:, None] * kz[None, :], NZ), 0)
+    slices = lambda order: (DEPTH * np.array(order)[:, None] + np.arange(DEPTH)[None, :]).reshape(NZ)
+    ahead = np.concatenate(turn(kz[:, None] * (slices(FORTH) - LAG)[None, :], NZ), 0)
+    back = np.concatenate(turn(slices(BACK)[:, None] * kz[None, :], NZ), 0)
     return ahead.astype(jnp.bfloat16), back.astype(jnp.bfloat16)
 
 
@@ -254,12 +261,12 @@
             blocks.append(whole[(k1 - 1) * 16 : k1 * 16, h * INNER : (h + 1) * INNER])
     for y in range(NY):
         for b in range(BLOCKS):
-            out_ref[RANK[y * BLOCKS + b]] = blocks[b][y * DEPTH : (y + 1) * DEPTH].astype(BF16)
+            out_ref[FORTH_RANK[y * BLOCKS + b]] = blocks[b][y * DEPTH : (y + 1) * DEPTH].astype(BF16)
 
 
 def inverse_kernel(in_ref, full_ref, ends_ref, twiddle_ref, out_ref):
     blocks = [
-        jnp.concatenate([in_ref[RANK[y * BLOCKS + b]].astype(F32) for y in range(NY)], 0).astype(BF16)
+        jnp.concatenate([in_ref[BACK_RANK[y * BLOCKS + b]].astype(F32) for y in range(NY)], 0).astype(BF16)
         for b in range(BLOCKS)
     ]
     even = dot(blocks[0], ends_ref[:, :INNER])
@@ -350,9 +357,9 @@
     )(*args)
 
 
-def exchange(chunks):
+def exchange(chunks, order):
     return lax.all_to_all(
-        chunks, "gz", split_axis=0, concat_axis=0, tiled=True, axis_index_groups=[list(ORDER)]
+        chunks, "gz", split_axis=0, concat_axis=0, tiled=True, axis_index_groups=[list(order)]
     )
 
 
@@ -395,12 +402,12 @@
         scratch=[pltpu.VMEM((3, 256, NX), BF16), pltpu.VMEM((3, 256, NX), BF16)],
         megabytes=24, flops=10**9,
     )
-    pencils = exchange(spectrum).reshape(NZ, INNER)
+    pencils = exchange(spectrum, FORTH).reshape(NZ, INNER)
     other = lax.ppermute(pencils, "half", [(i, i ^ 1) for i in range(lax.axis_size("half"))])
     returned = call(
         middle_kernel, shape(NZ, INNER), pencils, other, plus, minus, ahead, back,
     )
-    slabs = exchange(returned.reshape(GZ, DEPTH, INNER))
+    slabs = exchange(returned.reshape(GZ, DEPTH, INNER), BACK)
     residual = call(
         inverse_kernel, shape(DEPTH, NY, NX, dtype=F32), slabs, full_i, ends_i, twiddle,
     )

time: 52.3 us -> 50.9 us (0.973)
  blocking collectives: 29.4 us -> 28.4 us
    all_to_all x2, blocking collectives: 29.4 us -> 28.4 us  [exchange(): lax.all_to_all(chunks, 'gz', split_axis=0, concat_axis=0, tiled=True, axi...]
where the time goes in v5:
time: 50.9 us; the launch traced here: 50.7 us
  blocking collectives  28.4 us (56%)
  Pallas kernels  7.87 us (15%)
  starting transfers between devices  6.35 us (12%)
  waiting for transfers between devices  5.25 us (10%)
  other arithmetic  1.92 us (4%)
  local copies, waits for them, and re-layouts  0.79 us (2%)
    all_to_all x2, blocking collectives, exchange(): lax.all_to_all(chunks, 'gz', split_axis=0, concat_axis=0, tiled=True, axi...  28.4 us
    pallas_call x5, Pallas kernels, call(): pl.pallas_call(kernel, out_shape=outs, in_specs=[spec(pltpu.SMEM)] * smem...  7.87 us
    ppermute x1, waiting for transfers between devices, body(): left = lax.ppermute(rounded, 'gz', [(i, (i + 1) % GZ) for i in range(GZ)])  5.24 us
    ppermute x1, starting transfers between devices, body(): left = lax.ppermute(rounded, 'gz', [(i, (i + 1) % GZ) for i in range(GZ)])  3.9 us
    ppermute x1, starting transfers between devices, body(): lax.ppermute(pencils, 'half', [(i, i ^ 1) for i in range(lax.axis_size('h...  2.45 us
  transfers between devices with their start and end apart: 2, of which 1 were waited for; matrix products, arithmetic and copies ran while one was open for 3% of the time, Pallas kernels for 7%

profile of v5, /device:TPU:1, one launch (start us, length us, event | category | flops | bytes accessed | tf_op | source)
XLA Modules:
  0.0 50.7 jit_solution(5357512221024659645)
XLA Ops:
  0.0 0.9 %bitcast_convert_fusion.slab_ref = bf16[4,4,2048]{2,1,0:T(4,128)(2,1)S(1)} fusion(f32[1,4,4,2048]{3,2,1,0:T(4,128)} %param.16), kind=kLoop, calls=%fused_computation.1 | loop fusion | flops 32768 | bytes 196608 | tf_op jit(solution)/shard_map/convert_element_type | solution.py:385
  0.9 0.0 copy-start
  0.9 0.0 copy-start.4
  1.0 0.0 copy-start.5
  1.0 0.0 copy-start.7
  1.0 3.9 %collective-permute-start = (bf16[4,4,2048]{2,1,0:T(4,128)(2,1)S(1)}, bf16[4,4,2048]{2,1,0:T(4,128)(2,1)S(1)}, u32[]{:S(2)}, u32[]{:S(2)}) collective-permute-start(bf16[4,4,2048]{2,1,0:T(4,128)(2,1)S(1)} %bitcast_convert_fusion.slab_ref), channel_id=1, source_target_pairs={{0,1},{1,2},{2,3},{3,4},{4,5},{5,6},{6,7},{7,8},{8,9},{9,10},{10,1... | collective-permute-start | bytes 196616 | tf_op jit(solution)/shard_map/ppermute | solution.py:386
  4.9 1.0 %pad_maximum_fusion = bf16[32,16,3,3,3]{1,0,4,3,2:T(8,128)(2,1)S(1)} fusion(bf16[16,16,3,3,3]{1,0,4,3,2:T(8,128)(2,1)} %param.21, bf16[16,16,3,3,3]{1,0,4,3,2:T(8,128)(2,1)} %param.19), kind=kLoop, calls=%fused_computation | loop fusion | flops 55296 | bytes 55296 | tf_op jit(solution)/shard_map/concatenate | solution.py:390
  5.9 0.7 %stack.23.vector_ref = f32[5,16]{1,0:T(8,128)S(1)} concatenate(f32[1,16]{1,0:T(1,128)} %bitcast.19, f32[1,16]{1,0:T(1,128)} %bitcast.20, f32[1,16]{1,0:T(1,128)} %bitcast.21, f32[1,16]{1,0:T(1,128)} %bitcast.22, f32[1,16]{1,0:T(1,128)} %bitcast.23), dimensions={0} | concatenate | bytes 640 | tf_op jit(solution)/shard_map/stack | solution.py:389
  6.6 2.4 %shard_map.154 = (f32[5,64,128]{2,1,0:T(8,128)S(1)}, bf16[128,768]{1,0:T(8,128)(2,1)S(1)}, bf16[128,768]{1,0:T(8,128)(2,1)S(1)}, bf16[128,768]{1,0:T(8,128)(2,1)...) custom-call(s32[1]{0:T(128)} %bitcast.1.at_ref, ...), custom_call_target="tpu_custom_call" | custom-call | flops 1000000000 | bytes 93508 | tf_op jit(solution)/shard_map/pallas_call | solution.py:349
  9.1 5.2 %collective-permute-done.left_ref = bf16[4,4,2048]{2,1,0:T(4,128)(2,1)S(1)} collective-permute-done((bf16[4,4,2048]{2,1,0:T(4,128)(2,1)S(1)}, bf16[4,4,2048]{2,1,0:T(4,128)(2,1)S(1)}, u32[]{:S(2)}, u32[]{:S(2)}) %collective-permute-start) | collective-permute-done | bytes 65568 | tf_op jit(solution)/shard_map/ppermute | solution.py:386
  14.3 0.0 copy-done
  14.3 0.0 copy-done.4
  14.3 0.0 copy-done.5
  14.3 0.0 copy-done.7
  14.3 0.0 copy-start.8
  14.3 2.7 %shard_map.155 = bf16[64,4,128]{2,1,0:T(4,128)(2,1)S(1)} custom-call(bf16[4,4,2048]{2,1,0:T(4,128)(2,1)S(1)} %collective-permute-done.left_ref, f32[4,4,2048]{2,1,0:T(4,128)S(1)} %bitcast.14, f32[5,64,128]{2,1,0:T(8,128)S(1)} %get-tuple-element.14.par_ref, bf16[128,768]{1,0:T(8,128)(2,1)S(1)} %get-tuple-element.15.w1_ref, ...), custom_call_target="tpu_custom_call" | custom-call | flops 1000000000 | bytes 6070272 | tf_op jit(solution)/shard_map/pallas_call | solution.py:349
  17.0 0.0 copy-start.1
  17.0 0.0 copy-start.2
  17.0 14.0 %all_to_all.10 = bf16[64,4,128]{2,1,0:T(4,128)(2,1)S(1)} all-to-all(bf16[64,4,128]{2,1,0:T(4,128)(2,1)S(1)} %shard_map.155), channel_id=1, replica_groups={{34,47,16,38,36,54,4,52,51,48,45,20,7,50,30,49,44,15,58,35,10,9,55,25,1..., dimensions={0} | all-to-all | bytes 131072 | tf_op jit(solution)/shard_map/all_to_all | solution.py:361
  31.1 0.0 copy-start.3
  31.1 0.0 copy-start.6
  31.1 2.5 %collective-permute-start.1 = (bf16[256,128]{1,0:T(8,128)(2,1)S(1)}, bf16[256,128]{1,0:T(8,128)(2,1)S(1)}, u32[]{:S(2)}, u32[]{:S(2)}) collective-permute-start(bf16[256,128]{1,0:T(8,128)(2,1)S(1)} %bitcast.15), channel_id=1, source_target_pairs={{0,64},{64,0},{128,192},{192,128},{1,65},{65,1},{129,193},{193,129... | collective-permute-start | bytes 196616 | tf_op jit(solution)/shard_map/ppermute | solution.py:406
  33.6 0.0 copy-done.8
  33.6 1.2 %shard_map.156 = (f32[256,128]{1,0:T(8,128)S(1)}, f32[256,128]{1,0:T(8,128)S(1)}) custom-call(s32[1]{0:T(128)} %bitcast.1.at_ref, f32[256,2048]{1,0:T(8,128)S(1)} %copy-done.8), custom_call_target="tpu_custom_call" | custom-call | flops 1000000000 | bytes 2097156 | tf_op jit(solution)/shard_map/pallas_call | solution.py:349
  34.7 0.0 collective-permute-done.1.other_ref
  34.7 0.0 copy-done.1
  34.7 0.0 copy-done.2
  34.7 0.7 %shard_map.157 = bf16[256,128]{1,0:T(8,128)(2,1)S(1)} custom-call(bf16[256,128]{1,0:T(8,128)(2,1)S(1)} %bitcast.16, bf16[256,128]{1,0:T(8,128)(2,1)S(1)} %collective-permute-done.1.other_ref, f32[256,128]{1,0:T(8,128)S(1)} %get-tuple-element.21.plus_ref, f32[256,128]{1,0:T(8,128)S(1)} %get-tuple-element.22.minus_ref, bf16[512,256]{1,0:T(8,128)(2,1)S(1)} %copy-done.1, ...), custom_call_target="tpu_custom_call" | custom-call | flops 10000000 | bytes 917504 | tf_op jit(solution)/shard_map/pallas_call | solution.py:349
  35.4 14.4 %all_to_all.11.in_ref = bf16[64,4,128]{2,1,0:T(4,128)(2,1)S(1)} all-to-all(bf16[64,4,128]{2,1,0:T(4,128)(2,1)S(1)} %bitcast.17), channel_id=1, replica_groups={{42,58,26,38,46,22,62,41,10,30,34,43,54,47,50,6,57,25,14,27,45,37,39,59..., dimensions={0} | all-to-all | bytes 131072 | tf_op jit(solution)/shard_map/all_to_all | solution.py:361
  49.8 0.0 copy-done.3
  49.8 0.0 copy-done.6
  49.8 0.9 %shard_map.158 = f32[4,4,2048]{2,1,0:T(4,128)} custom-call(bf16[64,4,128]{2,1,0:T(4,128)(2,1)S(1)} %all_to_all.11.in_ref, bf16[256,256]{1,0:T(8,128)(2,1)S(1)} %copy-done.3, bf16[128,256]{1,0:T(8,128)(2,1)S(1)} %copy-done.6, f32[16,128]{1,0:T(8,128)S(1)} %copy-done.7), custom_call_target="tpu_custom_call" | custom-call | flops 10000000 | bytes 270336 | tf_op jit(solution)/shard_map/pallas_call | solution.py:349
Async XLA Ops:
  0.9 13.4 %copy-start = (f32[1,4,4,2048]{3,2,1,0:T(4,128)S(1)}, f32[1,4,4,2048]{3,2,1,0:T(4,128)}, u32[]{:S(2)}) copy-start(f32[1,4,4,2048]{3,2,1,0:T(4,128)} %param.16) | copy-start | bytes 393220
  0.9 13.4 %copy-start.4 = (bf16[256,256]{1,0:T(8,128)(2,1)S(1)}, bf16[256,256]{1,0:T(8,128)(2,1)}, u32[]{:S(2)}) copy-start(bf16[256,256]{1,0:T(8,128)(2,1)} %constant.18.clone.full_ref) | copy-start | bytes 393220
  1.0 13.4 %copy-start.5 = (bf16[128,256]{1,0:T(8,128)(2,1)S(1)}, bf16[128,256]{1,0:T(8,128)(2,1)}, u32[]{:S(2)}) copy-start(bf16[128,256]{1,0:T(8,128)(2,1)} %constant.19.clone.ends_ref) | copy-start | bytes 196612
  1.0 13.4 %copy-start.7 = (f32[16,128]{1,0:T(8,128)S(1)}, f32[16,128]{1,0:T(8,128)}, u32[]{:S(2)}) copy-start(f32[16,128]{1,0:T(8,128)} %constant.20.clone.twiddle_ref) | copy-start | bytes 24580
  1.0 13.3 %collective-permute-start = (bf16[4,4,2048]{2,1,0:T(4,128)(2,1)S(1)}, bf16[4,4,2048]{2,1,0:T(4,128)(2,1)S(1)}, u32[]{:S(2)}, u32[]{:S(2)}) collective-permute-start(bf16[4,4,2048]{2,1,0:T(4,128)(2,1)S(1)} %bitcast_convert_fusion.slab_ref), channel_id=1, source_target_pairs={{0,1},{1,2},{2,3},{3,4},{4,5},{5,6},{6,7},{7,8},{8,9},{9,10},{10,1... | collective-permute-start | bytes 196616 | tf_op jit(solution)/shard_map/ppermute | solution.py:386
  14.3 19.2 %copy-start.8 = (f32[256,2048]{1,0:T(8,128)S(1)}, f32[256,2048]{1,0:T(8,128)}, u32[]{:S(2)}) copy-start(f32[256,2048]{1,0:T(8,128)} %wedge_ref.1) | copy-start | bytes 6291460
  17.0 17.7 %copy-start.1 = (bf16[512,256]{1,0:T(8,128)(2,1)S(1)}, bf16[512,256]{1,0:T(8,128)(2,1)}, u32[]{:S(2)}) copy-start(bf16[512,256]{1,0:T(8,128)(2,1)} %constant.21.clone.ahead_ref) | copy-start | bytes 786436
  17.0 17.7 %copy-start.2 = (bf16[512,256]{1,0:T(8,128)(2,1)S(1)}, bf16[512,256]{1,0:T(8,128)(2,1)}, u32[]{:S(2)}) copy-start(bf16[512,256]{1,0:T(8,128)(2,1)} %constant.22.clone.back_ref) | copy-start | bytes 786436
  31.1 18.7 %copy-start.3 = (bf16[256,256]{1,0:T(8,128)(2,1)S(1)}, bf16[256,256]{1,0:T(8,128)(2,1)}, u32[]{:S(2)}) copy-start(bf16[256,256]{1,0:T(8,128)(2,1)} %constant.23.clone.full_ref) | copy-start | bytes 393220
  31.1 18.7 %copy-start.6 = (bf16[128,256]{1,0:T(8,128)(2,1)S(1)}, bf16[128,256]{1,0:T(8,128)(2,1)}, u32[]{:S(2)}) copy-start(bf16[128,256]{1,0:T(8,128)(2,1)} %constant.24.clone.ends_ref) | copy-start | bytes 196612
  31.1 3.6 %collective-permute-start.1 = (bf16[256,128]{1,0:T(8,128)(2,1)S(1)}, bf16[256,128]{1,0:T(8,128)(2,1)S(1)}, u32[]{:S(2)}, u32[]{:S(2)}) collective-permute-start(bf16[256,128]{1,0:T(8,128)(2,1)S(1)} %bitcast.15), channel_id=1, source_target_pairs={{0,64},{64,0},{128,192},{192,128},{1,65},{65,1},{129,193},{193,129... | collective-permute-start | bytes 196616 | tf_op jit(solution)/shard_map/ppermute | solution.py:406

commit v6 on v5

--- a/solution.py
+++ b/solution.py
@@ -143,7 +143,7 @@
         shifts(x_ref, row, x_ref[1, row : row + 16, :])
 
 
-CHUNK = 256
+CHUNK = 512
 
 
 def convolve(w_ref, parts, bias, at):

time: 50.9 us -> 50.8 us (level)
  no operation moved by 1% of the time
where the time goes in v6:
time: 50.8 us; the launch traced here: 50.6 us
  blocking collectives  28.4 us (56%)
  Pallas kernels  7.82 us (15%)
  starting transfers between devices  6.32 us (12%)
  waiting for transfers between devices  5.23 us (10%)
  other arithmetic  1.92 us (4%)
  local copies, waits for them, and re-layouts  0.79 us (2%)
    all_to_all x2, blocking collectives, exchange(): lax.all_to_all(chunks, 'gz', split_axis=0, concat_axis=0, tiled=True, axi...  28.4 us
    pallas_call x5, Pallas kernels, call(): pl.pallas_call(kernel, out_shape=outs, in_specs=[spec(pltpu.SMEM)] * smem...  7.82 us
    ppermute x1, waiting for transfers between devices, body(): left = lax.ppermute(rounded, 'gz', [(i, (i + 1) % GZ) for i in range(GZ)])  5.22 us
    ppermute x1, starting transfers between devices, body(): left = lax.ppermute(rounded, 'gz', [(i, (i + 1) % GZ) for i in range(GZ)])  3.9 us
    ppermute x1, starting transfers between devices, body(): lax.ppermute(pencils, 'half', [(i, i ^ 1) for i in range(lax.axis_size('h...  2.43 us
  transfers between devices with their start and end apart: 2, of which 1 were waited for; matrix products, arithmetic and copies ran while one was open for 3% of the time, Pallas kernels for 7%

profile of v6, /device:TPU:1, one launch (start us, length us, event | category | flops | bytes accessed | tf_op | source)
XLA Modules:
  0.0 50.6 jit_solution(11140551911549332711)
XLA Ops:
  0.0 0.9 %bitcast_convert_fusion.slab_ref = bf16[4,4,2048]{2,1,0:T(4,128)(2,1)S(1)} fusion(f32[1,4,4,2048]{3,2,1,0:T(4,128)} %param.16), kind=kLoop, calls=%fused_computation.1 | loop fusion | flops 32768 | bytes 196608 | tf_op jit(solution)/shard_map/convert_element_type | solution.py:385
  0.9 0.0 copy-start
  0.9 0.0 copy-start.4
  1.0 0.0 copy-start.5
  1.0 0.0 copy-start.7
  1.0 3.9 %collective-permute-start = (bf16[4,4,2048]{2,1,0:T(4,128)(2,1)S(1)}, bf16[4,4,2048]{2,1,0:T(4,128)(2,1)S(1)}, u32[]{:S(2)}, u32[]{:S(2)}) collective-permute-start(bf16[4,4,2048]{2,1,0:T(4,128)(2,1)S(1)} %bitcast_convert_fusion.slab_ref), channel_id=1, source_target_pairs={{0,1},{1,2},{2,3},{3,4},{4,5},{5,6},{6,7},{7,8},{8,9},{9,10},{10,1... | collective-permute-start | bytes 196616 | tf_op jit(solution)/shard_map/ppermute | solution.py:386
  4.9 1.0 %pad_maximum_fusion = bf16[32,16,3,3,3]{1,0,4,3,2:T(8,128)(2,1)S(1)} fusion(bf16[16,16,3,3,3]{1,0,4,3,2:T(8,128)(2,1)} %param.21, bf16[16,16,3,3,3]{1,0,4,3,2:T(8,128)(2,1)} %param.19), kind=kLoop, calls=%fused_computation | loop fusion | flops 55296 | bytes 55296 | tf_op jit(solution)/shard_map/concatenate | solution.py:390
  5.9 0.7 %stack.23.vector_ref = f32[5,16]{1,0:T(8,128)S(1)} concatenate(f32[1,16]{1,0:T(1,128)} %bitcast.19, f32[1,16]{1,0:T(1,128)} %bitcast.20, f32[1,16]{1,0:T(1,128)} %bitcast.21, f32[1,16]{1,0:T(1,128)} %bitcast.22, f32[1,16]{1,0:T(1,128)} %bitcast.23), dimensions={0} | concatenate | bytes 640 | tf_op jit(solution)/shard_map/stack | solution.py:389
  6.6 2.5 %shard_map.154 = (f32[5,64,128]{2,1,0:T(8,128)S(1)}, bf16[128,768]{1,0:T(8,128)(2,1)S(1)}, bf16[128,768]{1,0:T(8,128)(2,1)S(1)}, bf16[128,768]{1,0:T(8,128)(2,1)...) custom-call(s32[1]{0:T(128)} %bitcast.1.at_ref, ...), custom_call_target="tpu_custom_call" | custom-call | flops 1000000000 | bytes 93508 | tf_op jit(solution)/shard_map/pallas_call | solution.py:349
  9.1 5.2 %collective-permute-done.left_ref = bf16[4,4,2048]{2,1,0:T(4,128)(2,1)S(1)} collective-permute-done((bf16[4,4,2048]{2,1,0:T(4,128)(2,1)S(1)}, bf16[4,4,2048]{2,1,0:T(4,128)(2,1)S(1)}, u32[]{:S(2)}, u32[]{:S(2)}) %collective-permute-start) | collective-permute-done | bytes 65568 | tf_op jit(solution)/shard_map/ppermute | solution.py:386
  14.3 0.0 copy-done
  14.3 0.0 copy-done.4
  14.3 0.0 copy-done.5
  14.3 0.0 copy-done.7
  14.3 0.0 copy-start.8
  14.3 2.6 %shard_map.155 = bf16[64,4,128]{2,1,0:T(4,128)(2,1)S(1)} custom-call(bf16[4,4,2048]{2,1,0:T(4,128)(2,1)S(1)} %collective-permute-done.left_ref, f32[4,4,2048]{2,1,0:T(4,128)S(1)} %bitcast.14, f32[5,64,128]{2,1,0:T(8,128)S(1)} %get-tuple-element.14.par_ref, bf16[128,768]{1,0:T(8,128)(2,1)S(1)} %get-tuple-element.15.w1_ref, ...), custom_call_target="tpu_custom_call" | custom-call | flops 1000000000 | bytes 6070272 | tf_op jit(solution)/shard_map/pallas_call | solution.py:349
  16.9 0.0 copy-start.1
  17.0 0.0 copy-start.2
  17.0 14.1 %all_to_all.10 = bf16[64,4,128]{2,1,0:T(4,128)(2,1)S(1)} all-to-all(bf16[64,4,128]{2,1,0:T(4,128)(2,1)S(1)} %shard_map.155), channel_id=1, replica_groups={{34,47,16,38,36,54,4,52,51,48,45,20,7,50,30,49,44,15,58,35,10,9,55,25,1..., dimensions={0} | all-to-all | bytes 131072 | tf_op jit(solution)/shard_map/all_to_all | solution.py:361
  31.0 0.0 copy-start.3
  31.0 0.0 copy-start.6
  31.0 2.4 %collective-permute-start.1 = (bf16[256,128]{1,0:T(8,128)(2,1)S(1)}, bf16[256,128]{1,0:T(8,128)(2,1)S(1)}, u32[]{:S(2)}, u32[]{:S(2)}) collective-permute-start(bf16[256,128]{1,0:T(8,128)(2,1)S(1)} %bitcast.15), channel_id=1, source_target_pairs={{0,64},{64,0},{128,192},{192,128},{1,65},{65,1},{129,193},{193,129... | collective-permute-start | bytes 196616 | tf_op jit(solution)/shard_map/ppermute | solution.py:406
  33.5 0.0 copy-done.8
  33.5 1.2 %shard_map.156 = (f32[256,128]{1,0:T(8,128)S(1)}, f32[256,128]{1,0:T(8,128)S(1)}) custom-call(s32[1]{0:T(128)} %bitcast.1.at_ref, f32[256,2048]{1,0:T(8,128)S(1)} %copy-done.8), custom_call_target="tpu_custom_call" | custom-call | flops 1000000000 | bytes 2097156 | tf_op jit(solution)/shard_map/pallas_call | solution.py:349
  34.6 0.0 collective-permute-done.1.other_ref
  34.7 0.0 copy-done.1
  34.7 0.0 copy-done.2
  34.7 0.7 %shard_map.157 = bf16[256,128]{1,0:T(8,128)(2,1)S(1)} custom-call(bf16[256,128]{1,0:T(8,128)(2,1)S(1)} %bitcast.16, bf16[256,128]{1,0:T(8,128)(2,1)S(1)} %collective-permute-done.1.other_ref, f32[256,128]{1,0:T(8,128)S(1)} %get-tuple-element.21.plus_ref, f32[256,128]{1,0:T(8,128)S(1)} %get-tuple-element.22.minus_ref, bf16[512,256]{1,0:T(8,128)(2,1)S(1)} %copy-done.1, ...), custom_call_target="tpu_custom_call" | custom-call | flops 10000000 | bytes 917504 | tf_op jit(solution)/shard_map/pallas_call | solution.py:349
  35.4 14.4 %all_to_all.11.in_ref = bf16[64,4,128]{2,1,0:T(4,128)(2,1)S(1)} all-to-all(bf16[64,4,128]{2,1,0:T(4,128)(2,1)S(1)} %bitcast.17), channel_id=1, replica_groups={{42,58,26,38,46,22,62,41,10,30,34,43,54,47,50,6,57,25,14,27,45,37,39,59..., dimensions={0} | all-to-all | bytes 131072 | tf_op jit(solution)/shard_map/all_to_all | solution.py:361
  49.7 0.0 copy-done.3
  49.7 0.0 copy-done.6
  49.7 0.9 %shard_map.158 = f32[4,4,2048]{2,1,0:T(4,128)} custom-call(bf16[64,4,128]{2,1,0:T(4,128)(2,1)S(1)} %all_to_all.11.in_ref, bf16[256,256]{1,0:T(8,128)(2,1)S(1)} %copy-done.3, bf16[128,256]{1,0:T(8,128)(2,1)S(1)} %copy-done.6, f32[16,128]{1,0:T(8,128)S(1)} %copy-done.7), custom_call_target="tpu_custom_call" | custom-call | flops 10000000 | bytes 270336 | tf_op jit(solution)/shard_map/pallas_call | solution.py:349
Async XLA Ops:
  0.9 13.4 %copy-start = (f32[1,4,4,2048]{3,2,1,0:T(4,128)S(1)}, f32[1,4,4,2048]{3,2,1,0:T(4,128)}, u32[]{:S(2)}) copy-start(f32[1,4,4,2048]{3,2,1,0:T(4,128)} %param.16) | copy-start | bytes 393220
  0.9 13.4 %copy-start.4 = (bf16[256,256]{1,0:T(8,128)(2,1)S(1)}, bf16[256,256]{1,0:T(8,128)(2,1)}, u32[]{:S(2)}) copy-start(bf16[256,256]{1,0:T(8,128)(2,1)} %constant.18.clone.full_ref) | copy-start | bytes 393220
  1.0 13.4 %copy-start.5 = (bf16[128,256]{1,0:T(8,128)(2,1)S(1)}, bf16[128,256]{1,0:T(8,128)(2,1)}, u32[]{:S(2)}) copy-start(bf16[128,256]{1,0:T(8,128)(2,1)} %constant.19.clone.ends_ref) | copy-start | bytes 196612
  1.0 13.4 %copy-start.7 = (f32[16,128]{1,0:T(8,128)S(1)}, f32[16,128]{1,0:T(8,128)}, u32[]{:S(2)}) copy-start(f32[16,128]{1,0:T(8,128)} %constant.20.clone.twiddle_ref) | copy-start | bytes 24580
  1.0 13.3 %collective-permute-start = (bf16[4,4,2048]{2,1,0:T(4,128)(2,1)S(1)}, bf16[4,4,2048]{2,1,0:T(4,128)(2,1)S(1)}, u32[]{:S(2)}, u32[]{:S(2)}) collective-permute-start(bf16[4,4,2048]{2,1,0:T(4,128)(2,1)S(1)} %bitcast_convert_fusion.slab_ref), channel_id=1, source_target_pairs={{0,1},{1,2},{2,3},{3,4},{4,5},{5,6},{6,7},{7,8},{8,9},{9,10},{10,1... | collective-permute-start | bytes 196616 | tf_op jit(solution)/shard_map/ppermute | solution.py:386
  14.3 19.1 %copy-start.8 = (f32[256,2048]{1,0:T(8,128)S(1)}, f32[256,2048]{1,0:T(8,128)}, u32[]{:S(2)}) copy-start(f32[256,2048]{1,0:T(8,128)} %wedge_ref.1) | copy-start | bytes 6291460
  16.9 17.7 %copy-start.1 = (bf16[512,256]{1,0:T(8,128)(2,1)S(1)}, bf16[512,256]{1,0:T(8,128)(2,1)}, u32[]{:S(2)}) copy-start(bf16[512,256]{1,0:T(8,128)(2,1)} %constant.21.clone.ahead_ref) | copy-start | bytes 786436
  17.0 17.7 %copy-start.2 = (bf16[512,256]{1,0:T(8,128)(2,1)S(1)}, bf16[512,256]{1,0:T(8,128)(2,1)}, u32[]{:S(2)}) copy-start(bf16[512,256]{1,0:T(8,128)(2,1)} %constant.22.clone.back_ref) | copy-start | bytes 786436
  31.0 18.7 %copy-start.3 = (bf16[256,256]{1,0:T(8,128)(2,1)S(1)}, bf16[256,256]{1,0:T(8,128)(2,1)}, u32[]{:S(2)}) copy-start(bf16[256,256]{1,0:T(8,128)(2,1)} %constant.23.clone.full_ref) | copy-start | bytes 393220
  31.0 18.7 %copy-start.6 = (bf16[128,256]{1,0:T(8,128)(2,1)S(1)}, bf16[128,256]{1,0:T(8,128)(2,1)}, u32[]{:S(2)}) copy-start(bf16[128,256]{1,0:T(8,128)(2,1)} %constant.24.clone.ends_ref) | copy-start | bytes 196612
  31.0 3.6 %collective-permute-start.1 = (bf16[256,128]{1,0:T(8,128)(2,1)S(1)}, bf16[256,128]{1,0:T(8,128)(2,1)S(1)}, u32[]{:S(2)}, u32[]{:S(2)}) collective-permute-start(bf16[256,128]{1,0:T(8,128)(2,1)S(1)} %bitcast.15), channel_id=1, source_target_pairs={{0,64},{64,0},{128,192},{192,128},{1,65},{65,1},{129,193},{193,129... | collective-permute-start | bytes 196616 | tf_op jit(solution)/shard_map/ppermute | solution.py:406
